TPU v7x, 512 devices: a whole 4x8x8 slice. The times are simulated.
512 devices in a mesh: node: 16 (over y_lo, x, core), ctx: 32 (over y_hi, z).
Axes of the slice: x: 4, y: 8 (y_hi: 4, y_lo: 2; y = y_hi * 2 + y_lo), z: 8, core: 2. Of those that a mesh axis runs over, the one named last changes fastest.
Arguments:
- block_order: int32 [64], replicated, may hold values from 0 to 63, each once
- query_states: bfloat16 [4096, 4096], P('ctx', 'node'), may hold values from -11 to 11, as said below
- key_states: bfloat16 [4096, 512], P('ctx'), may hold values from -12 to 12, as said below
- value_states: bfloat16 [4096, 512], P('ctx'), may hold values from -4 to 4
- out_weight: bfloat16 [4096, 5120], P(('node', 'ctx')), may hold values from -0.09375 to 0.09375
- out_grad: bfloat16 [4096, 5120], P('ctx', 'node'), may hold values from -5 to 5
Outputs:
- attention: bfloat16 [4096, 4096], P('ctx', 'node')
- query_grad: bfloat16 [4096, 4096], P('ctx', 'node')
- key_grad: bfloat16 [4096, 512], P('ctx', 'node')
- value_grad: bfloat16 [4096, 512], P('ctx', 'node')
- weight_grad: bfloat16 [4096, 5120], P(('node', 'ctx'))
Inputs may be any that keep to these rules, and one draw needn't show every extreme that they name: `query_states`: entries are real numbers in the stated range. `key_states`: entries are real numbers in the stated range.
All inputs are finite; a program needn't handle non-finite values.
Results may differ from a plain program's by a relative error of at most 0.035.
Values may be sent and summed in bfloat16 or wider, within the bound.
A program may use at most 64 MiB of HBM per device.

v0:
```python
import math

import jax
import jax.numpy as jnp
from jax import lax
from jax.sharding import PartitionSpec as P

QH = 32
KVH = 4
HD = 128


def from_partner(shard, axis, stride):
    return lax.ppermute(shard, axis, [(i, i ^ 1 << stride) for i in range(lax.axis_size(axis))])


def row_positions(block_order, first_row, row_count, half_len):
    rows = first_row + lax.iota(jnp.int32, row_count)
    matches = (rows // half_len)[:, None] == lax.iota(jnp.int32, block_order.shape[0])[None, :]
    picked = jnp.sum(jnp.where(matches, block_order[None, :], 0), axis=1)
    return picked * half_len + rows % half_len


def blocked(update, running, row_count):
    span_rows = row_count
    while span_rows > 512 and span_rows % 2 == 0:
        span_rows = span_rows // 2
    return lax.fori_loop(
        0,
        row_count // span_rows,
        lambda number, current: update(current, number * span_rows, span_rows),
        running,
    )


def heads_major(rows_array, head_count):
    row_count = rows_array.shape[0]
    return (
        rows_array.reshape(row_count, head_count, -1)
        .transpose(1, 0, 2)
        .reshape(head_count * row_count, -1)
    )


def rows_major(stacked, head_count):
    row_count = stacked.shape[0] // head_count
    return stacked.reshape(head_count, row_count, -1).transpose(1, 0, 2).reshape(row_count, -1)


def halve_pairs(stacked, low_index, bit_count):
    current = stacked
    for bit in reversed(range(bit_count)):
        width = current.shape[2] // 2
        keeper = low_index // 2**bit % 2
        kept = lax.dynamic_slice_in_dim(current, keeper * width, width, 2)
        given = lax.dynamic_slice_in_dim(current, (1 - keeper) * width, width, 2)
        received = from_partner(given.astype(jnp.bfloat16), "node", bit).astype(given.dtype)
        current = kept + received
    return current


def per_device(block_order, query_states, key_states, value_states, out_weight, out_grad):
    local_rows = query_states.shape[0]
    half_len = local_rows // 2
    head_count = query_states.shape[1] // HD
    group_size = QH // KVH
    score_scale = 1.0 / math.sqrt(HD)
    highest = lax.Precision.HIGHEST
    kv_head = lax.axis_index("node") * head_count // group_size
    key_mine = lax.dynamic_slice_in_dim(key_states, kv_head * HD, HD, 1)
    value_mine = lax.dynamic_slice_in_dim(value_states, kv_head * HD, HD, 1)
    local_pos = row_positions(block_order, lax.axis_index("ctx") * local_rows, local_rows, half_len)
    query_pos = jnp.tile(local_pos, head_count)
    query_rows = heads_major(query_states, head_count)
    rows_total = head_count * local_rows
    start_state = (
        jnp.full((rows_total,), -1e30, jnp.float32),
        jnp.zeros((rows_total,), jnp.float32),
        jnp.zeros((rows_total, HD), jnp.float32),
    )
    key_part = lax.all_gather(key_mine, "ctx", axis=0, tiled=True)
    value_part = lax.all_gather(value_mine, "ctx", axis=0, tiled=True)

    def update(current, offset, span_rows):
        row_max, row_sum, weighted = current
        key_block = lax.dynamic_slice_in_dim(key_part, offset, span_rows, 0)
        value_block = lax.dynamic_slice_in_dim(value_part, offset, span_rows, 0).astype(jnp.float32)
        key_pos = row_positions(block_order, offset, span_rows, half_len)
        allowed = key_pos[None, :] <= query_pos[:, None]
        scores = (
            jnp.einsum("qd,kd->qk", query_rows, key_block, preferred_element_type=jnp.float32)
            * score_scale
        )
        new_max = jnp.maximum(row_max, jnp.max(jnp.where(allowed, scores, -1e30), axis=1))
        weights = jnp.where(allowed, jnp.exp(scores - new_max[:, None]), 0.0)
        factor = jnp.exp(row_max - new_max)
        row_sum = row_sum * factor + jnp.sum(weights, axis=1)
        weighted = weighted * factor[:, None] + jnp.dot(weights, value_block, precision=highest)
        return (new_max, row_sum, weighted)

    row_max, row_sum, weighted = blocked(update, start_state, key_part.shape[0])
    lse_rows = row_max + jnp.log(row_sum)
    attn_rows = (weighted / row_sum[:, None]).astype(jnp.bfloat16)
    attention = rows_major(attn_rows, head_count)
    full_grad = lax.all_gather(out_grad, "node", axis=1, tiled=True)
    weight_mine = lax.all_gather(out_weight, "ctx", axis=0, tiled=True)
    grad_attn = jnp.einsum(
        "td,hd->th", full_grad, weight_mine, preferred_element_type=jnp.float32
    ).astype(jnp.bfloat16)
    grad_rows = heads_major(grad_attn, head_count)
    row_dot = jnp.sum(grad_rows.astype(jnp.float32) * attn_rows.astype(jnp.float32), axis=1)
    weight_grad = lax.psum_scatter(
        jnp.einsum("th,td->hd", attention, full_grad, preferred_element_type=jnp.float32).astype(
            jnp.bfloat16
        ),
        "ctx",
        scatter_dimension=0,
        tiled=True,
    )
    lse_send = lse_rows.reshape(head_count, local_rows).T
    dot_send = row_dot.reshape(head_count, local_rows).T
    zero_query = jnp.zeros((rows_total, HD), jnp.float32)
    zero_key = jnp.zeros((local_rows, HD), jnp.float32)
    query_key_part = lax.all_gather(key_mine.astype(jnp.float32), "ctx", axis=0, tiled=True).astype(
        jnp.bfloat16
    )
    query_value_part = lax.all_gather(
        value_mine.astype(jnp.float32), "ctx", axis=0, tiled=True
    ).astype(jnp.bfloat16)

    def update(current, offset, span_rows):
        key_block = lax.dynamic_slice_in_dim(query_key_part, offset, span_rows, 0)
        value_block = lax.dynamic_slice_in_dim(query_value_part, offset, span_rows, 0)
        key_pos = row_positions(block_order, offset, span_rows, half_len)
        allowed = key_pos[None, :] <= query_pos[:, None]
        scores = (
            jnp.einsum("qd,kd->qk", query_rows, key_block, preferred_element_type=jnp.float32)
            * score_scale
        )
        softmax = jnp.where(allowed, jnp.exp(scores - lse_rows[:, None]), 0.0)
        grad_probs = jnp.einsum(
            "qd,kd->qk", grad_rows, value_block, preferred_element_type=jnp.float32
        )
        grad_scores = softmax * (grad_probs - row_dot[:, None])
        return (
            current
            + jnp.dot(grad_scores, key_block.astype(jnp.float32), precision=highest) * score_scale
        )

    query_sum = blocked(update, zero_query, query_key_part.shape[0])
    key_running = (zero_key, zero_key)
    query_part = lax.all_gather(query_states.astype(jnp.float32), "ctx", axis=0, tiled=True).astype(
        jnp.bfloat16
    )
    grad_part = lax.all_gather(grad_attn.astype(jnp.float32), "ctx", axis=0, tiled=True).astype(
        jnp.bfloat16
    )
    lse_part = lax.all_gather(lse_send, "ctx", axis=0, tiled=True)
    dot_part = lax.all_gather(dot_send, "ctx", axis=0, tiled=True)

    def update(current, offset, span_rows):
        key_acc, value_acc = current
        query_block = heads_major(
            lax.dynamic_slice_in_dim(query_part, offset, span_rows, 0), head_count
        )
        grad_block = heads_major(
            lax.dynamic_slice_in_dim(grad_part, offset, span_rows, 0), head_count
        )
        lse_block = heads_major(
            lax.dynamic_slice_in_dim(lse_part, offset, span_rows, 0), head_count
        ).reshape(-1)
        dot_block = heads_major(
            lax.dynamic_slice_in_dim(dot_part, offset, span_rows, 0), head_count
        ).reshape(-1)
        remote_pos = jnp.tile(row_positions(block_order, offset, span_rows, half_len), head_count)
        allowed = local_pos[None, :] <= remote_pos[:, None]
        scores = (
            jnp.einsum("qd,kd->qk", query_block, key_mine, preferred_element_type=jnp.float32)
            * score_scale
        )
        softmax = jnp.where(allowed, jnp.exp(scores - lse_block[:, None]), 0.0)
        value_acc = value_acc + jnp.einsum(
            "qk,qd->kd", softmax, grad_block.astype(jnp.float32), precision=highest
        )
        grad_probs = jnp.einsum(
            "qd,kd->qk", grad_block, value_mine, preferred_element_type=jnp.float32
        )
        grad_scores = softmax * (grad_probs - dot_block[:, None])
        key_acc = (
            key_acc
            + jnp.einsum(
                "qk,qd->kd", grad_scores, query_block.astype(jnp.float32), precision=highest
            )
            * score_scale
        )
        return (key_acc, value_acc)

    key_sum, value_sum = blocked(update, key_running, query_part.shape[0])
    key_acc = key_sum
    value_acc = value_sum
    query_grad = rows_major(query_sum.astype(jnp.bfloat16), head_count)
    sharers = group_size // head_count
    bit_count = sharers.bit_length() - 1
    low_index = lax.axis_index("node") % sharers
    summed = halve_pairs(jnp.stack([key_acc, value_acc]), low_index, bit_count)
    key_total = summed[0]
    value_total = summed[1]
    return (
        attention,
        query_grad,
        key_total.astype(jnp.bfloat16),
        value_total.astype(jnp.bfloat16),
        weight_grad,
    )


def solution(mesh):
    in_specs = (
        P(),
        P("ctx", "node"),
        P("ctx", None),
        P("ctx", None),
        P(("node", "ctx"), None),
        P("ctx", "node"),
    )
    out_specs = (
        P("ctx", "node"),
        P("ctx", "node"),
        P("ctx", "node"),
        P("ctx", "node"),
        P(("node", "ctx"), None),
    )
    return jax.shard_map(
        per_device, mesh=mesh, in_specs=in_specs, out_specs=out_specs, check_vma=False
    )
```

profile of v0, /device:TPU:6, one launch (start us, length us, event | category | flops | bytes accessed | tf_op | source)
XLA Modules:
  0.0 882.8 jit_solution(15060227893042610090)
XLA Ops:
  10.9 1.6 copy.39
  12.6 39.5 %all-gather.17.cloned.1.call-done = bf16[128,5120]{0,1:T(8,128)(2,1)} async-done(((bf16[128,320]{0,1:T(8,128)(2,1)}), bf16[128,5120]{0,1:T(8,128)(2,1)}) %all-gather.17.cloned.1.call-update) | async-done | bytes 1310736 | tf_op jit(solution)/shard_map/all_gather | solution.py:105
  52.0 93.7 %all-gather.19.cloned.1.call-done = bf16[256,5120]{1,0:T(8,128)(2,1)} async-done(((bf16[8,5120]{1,0:T(8,128)(2,1)}), bf16[256,5120]{1,0:T(8,128)(2,1)}) %all-gather.19.cloned.1.call-update) | async-done | bytes 2621456 | tf_op jit(solution)/shard_map/all_gather | solution.py:106
  145.7 3.8 convolution_convert_fusion.1
  151.9 76.8 %all-gather.11.cloned.1.call-done = bf16[4096,128]{1,0:T(8,128)(2,1)} async-done(((bf16[128,128]{1,0:T(8,128)(2,1)}), bf16[4096,128]{1,0:T(8,128)(2,1)}) %all-gather.11.cloned.1.call-update) | async-done | bytes 1048592 | tf_op jit(solution)/shard_map/all_gather | solution.py:82
  228.7 82.2 %all-gather.9.cloned.1.call-done = bf16[4096,128]{1,0:T(8,128)(2,1)} async-done(((bf16[128,128]{1,0:T(8,128)(2,1)}), bf16[4096,128]{1,0:T(8,128)(2,1)}) %all-gather.9.cloned.1.call-update) | async-done | bytes 1048592 | tf_op jit(solution)/shard_map/all_gather | solution.py:81
  310.9 30.3 %while.54 = (s32[]{:T(128)}, f32[256]{0:T(256)S(1)}, f32[256]{0:T(256)S(1)}, f32[256,128]{1,0:T(8,128)S(1)}, s32[64]{0:T(128)S(1)}, /*index=5*/bf16[4096,128]{1,...) while((s32[]{:T(128)}, f32[256]{0:T(256)S(1)}, ...), condition=%wide.region_5.6_spmd.clone, body=%wide.region_1.5_spmd.clone.sunk | while | flops 236535552 | bytes 2200519 | solution.py:28
  313.1 1.6 convolution_add_fusion.4
  316.9 1.6 convolution_add_fusion.4
  320.6 1.6 convolution_add_fusion.4
  324.4 1.6 convolution_add_fusion.4
  328.2 1.6 convolution_add_fusion.4
  332.0 1.6 convolution_add_fusion.4
  335.8 1.6 convolution_add_fusion.4
  339.6 1.6 convolution_add_fusion.4
  341.2 84.8 %all_gather.37 = f32[4096,2]{0,1:T(2,128)} all-gather(f32[128,2]{0,1:T(2,128)S(1)} %bitcast.164), channel_id=1, replica_groups=mesh['node'=16,'ctx'=32] {'ctx'}, dimensions={0}, use_global_device_ids=true | all-gather | bytes 33792 | tf_op jit(solution)/shard_map/all_gather | solution.py:158
  426.4 80.0 %all_gather.39 = f32[4096,2]{0,1:T(2,128)} all-gather(f32[128,2]{0,1:T(2,128)S(1)} %bitcast.163), channel_id=1, replica_groups=mesh['node'=16,'ctx'=32] {'ctx'}, dimensions={0}, use_global_device_ids=true | all-gather | bytes 33792 | tf_op jit(solution)/shard_map/all_gather | solution.py:159
  506.4 50.0 %while.56 = (s32[]{:T(128)}, f32[128,128]{1,0:T(8,128)S(1)}, f32[128,128]{1,0:T(8,128)S(1)}, s32[128]{0:T(128)}, s32[64]{0:T(128)S(1)}, /*index=5*/bf16[4096,256...) while((s32[]{:T(128)}, f32[128,128]{1,0:T(8,128)S(1)}, ...), condition=%wide.region_12.13_spmd.clone, body=%wide.region_10.12_spmd.clone.sunk | while | flops 470743552 | bytes 6689754 | solution.py:28
  556.7 2.9 collective-permute-start
  559.7 2.4 convolution_convert_fusion
  562.5 1.9 collective-permute-start.1
  564.5 81.1 %all-gather.15.cloned.1.call-done = bf16[4096,128]{1,0:T(8,128)(2,1)} async-done(((bf16[128,128]{1,0:T(8,128)(2,1)}), bf16[4096,128]{1,0:T(8,128)(2,1)}) %all-gather.15.cloned.1.call-update) | async-done | bytes 1048592 | tf_op jit(solution)/shard_map/all_gather | solution.py:127
  645.6 37.3 %while.55 = (s32[]{:T(128)}, f32[256,128]{1,0:T(8,128)S(1)}, s32[64]{0:T(128)S(1)}, bf16[4096,128]{1,0:T(8,128)(2,1)}, bf16[256,128]{1,0:T(8,128)(2,1)S(1)}, /*i...) while((s32[]{:T(128)}, f32[256,128]{1,0:T(8,128)S(1)}, ...), condition=%wide.region_9.10_spmd.clone, body=%wide.region_7.9_spmd.clone.sunk | while | flops 269433344 | bytes 2900945 | solution.py:28
  648.7 1.5 fusion.115
  653.4 1.5 fusion.115
  658.1 1.5 fusion.115
  662.7 1.5 fusion.115
  667.4 1.5 fusion.115
  672.1 1.5 fusion.115
  676.7 1.5 fusion.115
  681.4 1.5 fusion.115
  684.3 192.0 %reduce-scatter.2.cloned.1.call-done = bf16[8,5120]{1,0:T(8,128)(2,1)} async-done(((bf16[256,5120]{1,0:T(8,128)(2,1)}), bf16[8,5120]{1,0:T(8,128)(2,1)}) %reduce-scatter.2.cloned.1.call-update) | async-done | bytes 81936 | tf_op jit(solution)/shard_map/reduce_scatter | solution.py:112
  (323 shorter events, 99.1 us)
Async XLA Ops:
  7.2 1.6 copy-start
  7.2 44.9 %all-gather.17.cloned.1.call-start = ((), (), s32[]{:S(2)}) async-start(), calls=%async_computation.5 | async-start | bytes 1392640 | tf_op jit(solution)/shard_map/all_gather | solution.py:105
  7.9 137.8 %all-gather.19.cloned.1.call-start = ((), (), s32[]{:S(2)}) async-start(), calls=%async_computation.6 | async-start | bytes 2703360 | tf_op jit(solution)/shard_map/all_gather | solution.py:106
  8.7 220.0 %all-gather.11.cloned.1.call-start = ((), (), s32[]{:S(2)}) async-start(), calls=%async_computation.2 | async-start | bytes 1081344 | tf_op jit(solution)/shard_map/all_gather | solution.py:82
  9.4 301.5 %all-gather.9.cloned.1.call-start = ((), (), s32[]{:S(2)}) async-start(), calls=%async_computation.1 | async-start | bytes 1081344 | tf_op jit(solution)/shard_map/all_gather | solution.py:81
  10.8 495.6 %all-gather.21.cloned.1.call-start = ((), (), s32[]{:S(2)}) async-start(), calls=%async_computation.7 | async-start | bytes 2162688 | tf_op jit(solution)/shard_map/all_gather | solution.py:152
  12.5 138.6 %copy-start.6 = (bf16[128,256]{1,0:T(8,128)(2,1)S(1)}, bf16[128,256]{1,0:T(8,128)(2,1)}, u32[]{:S(2)}) copy-start(bf16[128,256]{1,0:T(8,128)(2,1)} %param.13) | copy-start | bytes 196612
  12.5 138.8 %copy-start.7 = (s32[64]{0:T(128)S(1)}, s32[64]{0:T(128)}, u32[]{:S(2)}) copy-start(s32[64]{0:T(128)} %param.12) | copy-start | bytes 772
  12.5 493.9 %all-gather.23.cloned.1.call-start = ((), (), s32[]{:S(2)}) async-start(), calls=%async_computation.8 | async-start | bytes 2162688 | tf_op jit(solution)/shard_map/all_gather | solution.py:155
  149.6 414.9 %all-gather.13.cloned.1.call-start = ((), (), s32[]{:S(2)}) async-start(), calls=%async_computation.3 | async-start | bytes 1081344 | tf_op jit(solution)/shard_map/all_gather | solution.py:124
  150.3 495.3 %all-gather.15.cloned.1.call-start = ((), (), s32[]{:S(2)}) async-start(), calls=%async_computation.4 | async-start | bytes 1081344 | tf_op jit(solution)/shard_map/all_gather | solution.py:127
  151.1 725.2 %reduce-scatter.2.cloned.1.call-start = ((), (), s32[]{:S(2)}) async-start(), calls=%async_computation.9 | async-start | bytes 2703360 | tf_op jit(solution)/shard_map/reduce_scatter | solution.py:112
  310.9 115.1 %copy-start.3 = (bf16[128,256]{1,0:T(8,128)(2,1)S(1)}, bf16[128,256]{1,0:T(8,128)(2,1)}, u32[]{:S(2)}) copy-start(bf16[128,256]{1,0:T(8,128)(2,1)} %convolution_convert_fusion.1) | copy-start | bytes 196612
  310.9 195.5 %copy-start.2 = (bf16[128,128]{1,0:T(8,128)(2,1)S(1)}, bf16[128,128]{1,0:T(8,128)(2,1)}, u32[]{:S(2)}) copy-start(bf16[128,128]{1,0:T(8,128)(2,1)} %constant_dynamic-slice_fusion.2) | copy-start | bytes 98308
  310.9 195.5 %copy-start.4 = (bf16[128,128]{1,0:T(8,128)(2,1)S(1)}, bf16[128,128]{1,0:T(8,128)(2,1)}, u32[]{:S(2)}) copy-start(bf16[128,128]{1,0:T(8,128)(2,1)} %constant_dynamic-slice_fusion.3) | copy-start | bytes 98308
  426.4 133.3 %copy-start.5 = (bf16[16,8,2,128]{3,1,2,0:T(8,128)(2,1)}, bf16[16,8,2,128]{3,1,2,0:T(8,128)(2,1)S(1)}, u32[]{:S(2)}) copy-start(bf16[16,8,2,128]{3,1,2,0:T(8,128)(2,1)S(1)} %copy.54) | copy-start | bytes 196612
  506.4 53.2 %copy-start.1 = (bf16[128,5120]{0,1:T(8,128)(2,1)S(1)}, bf16[128,5120]{0,1:T(8,128)(2,1)}, u32[]{:S(2)}) copy-start(bf16[128,5120]{0,1:T(8,128)(2,1)} %all-gather.17.cloned.1.call-done) | copy-start | bytes 3932164
  556.7 5.8 collective-permute-start
  562.5 121.1 %collective-permute-start.1 = (bf16[2,128,32]{1,2,0:T(8,128)(2,1)S(1)}, bf16[2,128,32]{1,2,0:T(8,128)(2,1)S(1)}, u32[]{:S(2)}, u32[]{:S(2)}) collective-permute-start(bf16[2,128,32]{1,2,0:T(8,128)(2,1)S(1)} %dynamic-slice_convert_fusion), channel_id=1, source_target_pairs={{0,32},{32,0},{64,96},{96,64},{128,160},{160,128},{192,224},{224,1... | collective-permute-start | bytes 49160 | tf_op jit(solution)/shard_map/ppermute | solution.py:14
Sparse Core Ops, SparseCore 0:
  10.2 41.8 all-gather.16
  55.2 90.5 all-gather.18
  148.9 79.7 all-gather.10
  231.7 79.1 all-gather.8
  314.4 82.3 all-gather.20
  400.4 80.2 all-gather.22
  483.9 79.3 all-gather.12
  566.4 79.1 all-gather.14
  650.6 225.6 reduce-scatter.1
where the time goes:
time: 885 us; the launch traced here: 883 us
  waiting for transfers between devices  569 us (64%)
  blocking collectives  165 us (19%)
  matrix products  82.1 us (9%)
  local copies, waits for them, and re-layouts  40.9 us (5%)
  between operations  14.2 us (2%)
    reduce_scatter x1, waiting for transfers between devices, per_device(): lax.psum_scatter(jnp.einsum('th,td->hd', attention, full_grad, preferred_...  192 us
    all_gather x1, waiting for transfers between devices, per_device(): weight_mine = lax.all_gather(out_weight, 'ctx', axis=0, tiled=True)  93.7 us
    all_gather x1, blocking collectives, per_device(): lse_part = lax.all_gather(lse_send, 'ctx', axis=0, tiled=True)  84.8 us
    all_gather x1, waiting for transfers between devices, per_device(): key_part = lax.all_gather(key_mine, 'ctx', axis=0, tiled=True)  82.2 us
    all_gather x1, waiting for transfers between devices, per_device(): lax.all_gather(value_mine.astype(jnp.float32), 'ctx', axis=0, tiled=True)  81.1 us
    all_gather x1, blocking collectives, per_device(): dot_part = lax.all_gather(dot_send, 'ctx', axis=0, tiled=True)  80 us
    all_gather x1, waiting for transfers between devices, per_device(): value_part = lax.all_gather(value_mine, 'ctx', axis=0, tiled=True)  76.8 us
    all_gather x1, waiting for transfers between devices, per_device(): full_grad = lax.all_gather(out_grad, 'node', axis=1, tiled=True)  39.5 us
  transfers between devices with their start and end apart: 11, of which 7 were waited for; matrix products, arithmetic and copies ran while one was open for 15% of the time, Pallas kernels for 0%

commit v1 on v0

v1 whole, which is shorter than its diff:
```python
import functools
import math

import jax
import jax.numpy as jnp
from jax import lax
from jax.experimental import pallas as pl
from jax.experimental.pallas import tpu as pltpu
from jax.sharding import PartitionSpec as P

HD = 128
TOK = 128
NEG = -1e30
SCALE = 1.0 / math.sqrt(HD)
LOG2E = math.log2(math.e)
F32 = jnp.float32
BF16 = jnp.bfloat16
MESH = pl.DeviceIdType.MESH

OFFSET = (4, 5, 3, 6, 2, 7, 1, 0)
RIGHT_SLOT = (5, 3, 1, 0)
LEFT_SLOT = (6, 4, 2)


def nn(a, b):
    return lax.dot_general(a, b, (((1,), (0,)), ((), ())), preferred_element_type=F32)


def nt(a, b):
    return lax.dot_general(a, b, (((1,), (1,)), ((), ())), preferred_element_type=F32)


def fold8(a):
    return a.reshape(a.shape[0] // 8, 8, a.shape[1])


class Sems:
    def __init__(self, send, recv):
        self.send, self.recv, self.used = send, recv, 0

    def take(self, count):
        base = self.used
        self.used += count
        return base

    def copy(self, src, dst, sid, rid, node, ctx):
        return pltpu.make_async_remote_copy(
            src_ref=src,
            dst_ref=dst,
            send_sem=self.send.at[sid],
            recv_sem=self.recv.at[rid],
            device_id={"node": node, "ctx": ctx},
            device_id_type=MESH,
        )


SEM_COUNT = 96


def kernel(
    order_ref, q_ref, k_ref, v_ref, w_ref, og_ref,
    attn_ref, dq_ref, dk_ref, dv_ref, dw_ref,
    kvg, kv, qbuf, qall, krel, vrel, kt, vt,
    wsl, wring, w32, ogt, dot2,
    sp, mx, pb, dsb, mloc,
    osend, obuf, ostat, ostatbuf,
    at, gpart, gpsend, gpbuf, gown, gbuf, gstat, gstatbuf, gtall, frow, drow,
    smp, rsend_r, rsend_l, rrecv_r, rrecv_l, kvfin_send, kvfin,
    dqsend, dqbuf, dqown,
    dwp, wsend_r, wsend_l, wrecv_r, wrecv_l, dwsend, dwfin,
    send_sem, recv_sem,
):
    node = lax.axis_index("node")
    ctx = lax.axis_index("ctx")
    core = lax.rem(node, 2)
    x = lax.rem(node // 2, 4)
    ylo = node // 8
    g = node // 4
    m = lax.rem(node, 4)
    yhi = ctx // 8
    z = lax.rem(ctx, 8)

    sems = Sems(send_sem, recv_sem)
    pending = []

    def y_peer(k):
        return node, lax.rem(yhi + k, 4) * 8 + z

    def group_peer(k):
        return g * 4 + lax.rem(m + k, 4), ctx

    z_right = (node, yhi * 8 + lax.rem(z + 1, 8))
    z_left = (node, yhi * 8 + lax.rem(z + 7, 8))
    x_right = ((ylo * 4 + lax.rem(x + 1, 4)) * 2 + core, ctx)
    x_left = ((ylo * 4 + lax.rem(x + 3, 4)) * 2 + core, ctx)
    y_flip = (((1 - ylo) * 4 + x) * 2 + core, ctx)
    sibling = (node + 1 - 2 * core, ctx)
    turned = ((ylo * 4 + yhi) * 2 + core, x * 8 + z)

    barrier = pltpu.get_barrier_semaphore()

    def greet(peer):
        pl.semaphore_signal(
            barrier, inc=1, device_id={"node": peer[0], "ctx": peer[1]}, device_id_type=MESH
        )

    for k in range(1, 4):
        greet(y_peer(k))
        greet(group_peer(k))
    for peer in (z_right, z_left, x_right, x_left, y_flip):
        greet(peer)

    @pl.when(x != yhi)
    def _():
        greet(turned)

    @pl.when(m != yhi)
    def _():
        for k in range(1, 4):
            greet((g * 4 + yhi, lax.rem(yhi + k, 4) * 8 + z))

    glane = pl.ds(pl.multiple_of(g * HD, HD), HD)
    kvg[0] = k_ref[:, glane]
    kvg[1] = v_ref[:, glane]
    w_rows = w_ref[...].astype(F32)
    for q in range(4):
        slabs = []
        for j in range(10):
            col = 2560 * (j // 5) + 640 * q + 128 * (j % 5)
            slabs.append(w_rows[:, col : col + 128])
        wsl[q] = jnp.concatenate(slabs, axis=0).astype(BF16)
    eye = (
        lax.broadcasted_iota(jnp.int32, (320, 320), 0)
        == lax.broadcasted_iota(jnp.int32, (320, 320), 1)
    ).astype(F32).astype(BF16)
    ogt[...] = nt(eye, og_ref[...]).astype(BF16)

    pl.semaphore_wait(
        barrier, 11 + jnp.where(x != yhi, 1, 0) + jnp.where(m != yhi, 3, 0)
    )

    kv_hop = sems.take(4)
    kv_hop_copies = [
        sems.copy(kvg, kv.at[7], kv_hop + k, kv_hop, *y_peer(k)) for k in range(1, 4)
    ]

    @pl.when(m == yhi)
    def _():
        for copy in kv_hop_copies:
            copy.start()

    q_sem = sems.take(4)
    q_copies = [
        sems.copy(q_ref, qbuf.at[k], q_sem + k, q_sem + k, *group_peer(k)) for k in range(1, 4)
    ]
    for copy in q_copies:
        copy.start()
    pending += q_copies

    def dot_rows(lo, co):
        return pl.ds(pl.multiple_of((lo * 2 + co) * 320, 64), 320)

    def dot_lanes(position):
        return pl.ds(pl.multiple_of(position * TOK, TOK), TOK)

    turn_sem = sems.take(1)
    turn_copy = sems.copy(
        ogt, dot2.at[dot_rows(ylo, core), dot_lanes(yhi)], turn_sem, turn_sem, *turned
    )

    @pl.when(x != yhi)
    def _():
        turn_copy.start()

    @pl.when(x == yhi)
    def _():
        dot2[dot_rows(ylo, core), dot_lanes(yhi)] = ogt[...]

    w_sem = sems.take(4)
    w_copies = []
    for k in range(1, 4):
        peer = y_peer(k)
        w_copies.append(
            sems.copy(
                wsl.at[lax.rem(yhi + k, 4)], wring.at[7, yhi], w_sem + k, w_sem + k, *peer
            )
        )
        w_copies[-1].start()
    pending += w_copies
    wring[7, yhi] = wsl[yhi]

    def ring(buffer):
        base = sems.take(7)
        rights = [
            sems.copy(
                buffer.at[7 if s == 0 else RIGHT_SLOT[s - 1]],
                buffer.at[RIGHT_SLOT[s]],
                base + s,
                base + s,
                *z_right,
            )
            for s in range(4)
        ]
        lefts = [
            sems.copy(
                buffer.at[7 if s == 0 else LEFT_SLOT[s - 1]],
                buffer.at[LEFT_SLOT[s]],
                base + 4 + s,
                base + 4 + s,
                *z_left,
            )
            for s in range(3)
        ]
        return rights, lefts

    def ring_step(rings, s):
        rights, lefts = rings
        if s > 0:
            rights[s - 1].wait_recv()
            if s < 4:
                lefts[s - 1].wait_recv()
        if s < 4:
            rights[s].start()
            pending.append(rights[s])
        if s < 3:
            lefts[s].start()
            pending.append(lefts[s])

    kv_ring = ring(kv)
    w_ring = ring(wring)

    @pl.when(m == yhi)
    def _():
        kv[7] = kvg[...]

    @pl.when(m != yhi)
    def _():
        sems.copy(kvg, kv.at[7], kv_hop, kv_hop, *y_peer(1)).wait_recv()

    ring_step(kv_ring, 0)

    @pl.when(x != yhi)
    def _():
        turn_copy.wait_recv()

    flip_sem = sems.take(1)
    own_block = dot2.at[dot_rows(ylo, core), dot_lanes(x)]
    flip_copy = sems.copy(own_block, own_block, flip_sem, flip_sem, *y_flip)
    flip_copy.start()
    pending.append(flip_copy)

    for copy in w_copies:
        copy.wait_recv()
    ring_step(w_ring, 0)

    qbuf[0] = q_ref[...]
    for copy in q_copies:
        copy.wait_recv()
    for r in range(4):
        for h in range(2):
            qall[r * 256 + h * 128 : r * 256 + h * 128 + 128, :] = qbuf[
                r, :, h * 128 : h * 128 + 128
            ]

    def place(first_block, dim):
        index = lax.broadcasted_iota(jnp.int32, (TOK, TOK), dim)
        low = order_ref[first_block] * 64 + index
        high = order_ref[first_block + 1] * 64 + (index - 64)
        return jnp.where(index < 64, low, high)

    query_place = place(ctx * 2, 1)
    mx[...] = jnp.full(mx.shape, NEG, F32)

    def score_block(slot):
        block = m * 8 + lax.rem(z + OFFSET[slot], 8)
        allowed = place(block * 2, 0) <= query_place
        allowed = jnp.concatenate([allowed, allowed], axis=1)
        rows = slice(slot * 128, slot * 128 + 128)
        keys = kv[slot, 0]
        values = kv[slot, 1]
        krel[rows, :] = keys
        vrel[rows, :] = values
        kt[:, rows] = keys.astype(F32).T.astype(BF16)
        vt[:, rows] = values.astype(F32).T.astype(BF16)
        for r in range(4):
            lanes = slice(r * 256, r * 256 + 256)
            scores = nt(keys, qall[lanes, :]) * (SCALE * LOG2E)
            scores = jnp.where(allowed, scores, NEG)
            sp[rows, lanes] = scores
            mx[:, lanes] = jnp.maximum(mx[:, lanes], jnp.max(fold8(scores), axis=0))

    score_block(7)

    ring_step(kv_ring, 1)
    flip_copy.wait_recv()
    x_sem = sems.take(6)
    x_first = []
    for lo in range(2):
        block = dot2.at[dot_rows(lo, core), dot_lanes(x)]
        x_first.append(sems.copy(block, block, x_sem + lo, x_sem + lo, *x_right))
        x_first.append(sems.copy(block, block, x_sem + 2 + lo, x_sem + 2 + lo, *x_left))
    for copy in x_first:
        copy.start()
    pending += x_first
    score_block(5)
    score_block(6)
    ring_step(w_ring, 1)

    ring_step(kv_ring, 2)
    score_block(3)
    score_block(4)
    for copy in x_first:
        copy.wait_recv()
    from_left = dot2.at[dot_rows(0, core), dot_lanes(lax.rem(x + 3, 4))]
    from_right = dot2.at[dot_rows(1, core), dot_lanes(lax.rem(x + 1, 4))]
    x_second = [
        sems.copy(from_left, from_left, x_sem + 4, x_sem + 4, *x_right),
        sems.copy(from_right, from_right, x_sem + 5, x_sem + 5, *x_left),
    ]
    for copy in x_second:
        copy.start()
    pending += x_second
    ring_step(w_ring, 2)

    ring_step(kv_ring, 3)
    score_block(1)
    score_block(2)
    for copy in x_second:
        copy.wait_recv()
    core_sem = sems.take(2)
    core_copies = []
    for lo in range(2):
        half = dot2.at[dot_rows(lo, core), :]
        core_copies.append(sems.copy(half, half, core_sem + lo, core_sem + lo, *sibling))
        core_copies[-1].start()
    pending += core_copies
    ring_step(w_ring, 3)

    ring_step(kv_ring, 4)
    score_block(0)

    o_sem = sems.take(8)
    o_copies = []

    def forward(r):
        lanes = slice(r * 256, r * 256 + 256)
        row_max = jnp.maximum(jnp.max(mx[:, lanes], axis=0, keepdims=True), -1e20)

        def body(i, total):
            rows = pl.ds(pl.multiple_of(i * 128, 128), 128)
            weights = jnp.exp2(sp[rows, lanes] - row_max)
            sp[rows, lanes] = weights
            pb[rows, lanes] = weights.astype(BF16)
            return total + jnp.sum(fold8(weights), axis=0)

        total = lax.fori_loop(0, 8, body, jnp.zeros((8, 256), F32))
        row_sum = jnp.sum(total, axis=0, keepdims=True)
        mloc[:, lanes] = row_max
        return row_max, row_sum, nn(vt[...], pb[:, lanes])

    def stat_rows(first, second):
        index = lax.broadcasted_iota(jnp.int32, (8, 256), 0)
        return jnp.where(index == 0, first, second)

    for r in (1, 2, 3):
        row_max, row_sum, part = forward(r)
        osend[r] = part.astype(BF16)
        ostat[r] = stat_rows(row_max, row_sum)
        k = 4 - r
        peer = group_peer(k)
        o_copies.append(sems.copy(osend.at[r], obuf.at[k], o_sem + k, o_sem + k, *peer))
        o_copies.append(
            sems.copy(ostat.at[r], ostatbuf.at[k], o_sem + 4 + k, o_sem + 4 + k, *peer)
        )
        o_copies[-2].start()
        o_copies[-1].start()
    pending += o_copies
    own_max, own_sum, own_part = forward(0)
    obuf_own = own_part

    ring_step(w_ring, 4)
    for slot in range(8):
        first = lax.rem(z + OFFSET[slot], 8) * 8
        for y in range(4):
            block = wring[slot, y].astype(F32)
            rows = pl.ds(pl.multiple_of(first + y * 64, 8), 8)
            for j in range(10):
                w32[rows, j * 128 : j * 128 + 128] = block[j * 8 : j * 8 + 8, :]
    for copy in core_copies:
        copy.wait_recv()
    weight = w32[...].astype(BF16)
    gpart[...] = nn(weight, dot2[...])
    gp_sem = sems.take(4)
    gp_copies = []
    for k in range(1, 4):
        gpsend[k] = gpart[:, dot_lanes(lax.rem(yhi + k, 4))].astype(BF16)
        gp_copies.append(
            sems.copy(gpsend.at[k], gpbuf.at[k], gp_sem + k, gp_sem + k, *y_peer(k))
        )
        gp_copies[-1].start()
    pending += gp_copies

    for copy in o_copies:
        copy.wait_recv()
    maxes = [own_max] + [ostatbuf[k, 0:1, :] for k in range(1, 4)]
    sums = [own_sum] + [ostatbuf[k, 1:2, :] for k in range(1, 4)]
    parts = [obuf_own] + [obuf[k].astype(F32) for k in range(1, 4)]
    top = functools.reduce(jnp.maximum, maxes)
    factors = [jnp.exp2(value - top) for value in maxes]
    total = sum(f * s for f, s in zip(factors, sums))
    attention = sum(f * p for f, p in zip(factors, parts)) / total
    lse = top + jnp.log2(total)
    attention_rows = jnp.concatenate([attention[:, :128], attention[:, 128:]], axis=0)
    attention_bf = attention_rows.astype(BF16)
    my_lanes = dot_lanes(yhi)
    at[:, my_lanes] = attention_bf
    at_sem = sems.take(4)
    at_copies = []
    for k in range(1, 4):
        mine = at.at[:, my_lanes]
        at_copies.append(sems.copy(mine, mine, at_sem + k, at_sem + k, *y_peer(k)))
        at_copies[-1].start()
    pending += at_copies
    attn_ref[...] = attention_rows.T.astype(BF16)

    for copy in gp_copies:
        copy.wait_recv()
    grad = gpart[:, my_lanes]
    for k in range(1, 4):
        grad = grad + gpbuf[k].astype(F32)
    grad_bf = grad.astype(BF16)
    gown[...] = grad_bf
    products = grad_bf.astype(F32) * attention_bf.astype(F32)
    row_dot = jnp.concatenate(
        [
            jnp.sum(products[:128], axis=0, keepdims=True),
            jnp.sum(products[128:], axis=0, keepdims=True),
        ],
        axis=1,
    )
    own_stat = stat_rows(lse, row_dot)
    gstat[...] = own_stat
    g_sem = sems.take(8)
    g_copies = []
    for k in range(1, 4):
        peer = group_peer(k)
        g_copies.append(sems.copy(gown, gbuf.at[k], g_sem + k, g_sem + k, *peer))
        g_copies.append(
            sems.copy(gstat, gstatbuf.at[k], g_sem + 4 + k, g_sem + 4 + k, *peer)
        )
        g_copies[-2].start()
        g_copies[-1].start()
    pending += g_copies

    for copy in at_copies:
        copy.wait_recv()
    dwp[...] = nt(at[...], dot2[...])

    def weight_block(slot):
        first = lax.rem(z + OFFSET[slot], 8) * 8
        slabs = []
        for y in range(4):
            rows = pl.ds(pl.multiple_of(first + y * 64, 8), 8)
            for j in range(10):
                slabs.append(dwp[rows, j * 128 : j * 128 + 128])
        return jnp.concatenate(slabs, axis=0)

    def sum_ring(sends_r, recvs_r, sends_l, recvs_l):
        base = sems.take(7)
        rights = [
            sems.copy(sends_r.at[s], recvs_r.at[s], base + s, base + s, *z_right)
            for s in range(4)
        ]
        lefts = [
            sems.copy(sends_l.at[s], recvs_l.at[s], base + 4 + s, base + 4 + s, *z_left)
            for s in range(3)
        ]
        return rights, lefts

    dw_rights, dw_lefts = sum_ring(wsend_r, wrecv_r, wsend_l, wrecv_l)

    def weight_step(s):
        right = weight_block(2 * s)
        if s > 0:
            dw_rights[s - 1].wait_recv()
            right = right + wrecv_r[s - 1].astype(F32)
        wsend_r[s] = right.astype(BF16)
        dw_rights[s].start()
        pending.append(dw_rights[s])
        if s < 3:
            left = weight_block(2 * s + 1)
            if s > 0:
                dw_lefts[s - 1].wait_recv()
                left = left + wrecv_l[s - 1].astype(F32)
            wsend_l[s] = left.astype(BF16)
            dw_lefts[s].start()
            pending.append(dw_lefts[s])

    weight_step(0)

    for copy in g_copies:
        copy.wait_recv()
    for r in range(4):
        block = gown[...] if r == 0 else gbuf[r]
        for h in range(2):
            gtall[:, r * 256 + h * 128 : r * 256 + h * 128 + 128] = block[
                h * 128 : h * 128 + 128, :
            ]
        stat = own_stat if r == 0 else gstatbuf[r]
        lanes = slice(r * 256, r * 256 + 256)
        frow[:, lanes] = jnp.exp2(mloc[:, lanes] - stat[0:1, :])
        drow[:, lanes] = stat[1:2, :]

    kv_rights, kv_lefts = sum_ring(rsend_r, rrecv_r, rsend_l, rrecv_l)

    def backward(s):
        rows = slice(s * 256, s * 256 + 256)
        values = vrel[rows, :]
        for r in range(4):
            lanes = slice(r * 256, r * 256 + 256)
            grad_probs = nn(values, gtall[:, lanes])
            softmax = sp[rows, lanes] * frow[:, lanes]
            smp[:, lanes] = softmax.astype(BF16)
            dsb[rows, lanes] = (softmax * (grad_probs - drow[:, lanes])).astype(BF16)
        key_part = nn(dsb[rows, :], qall[...]) * SCALE
        value_part = nt(smp[...], gtall[...])
        return key_part, value_part

    own_key = own_value = None
    for s in range(4):
        key_part, value_part = backward(s)
        right_key, right_value = key_part[:128], value_part[:128]
        left_key, left_value = key_part[128:], value_part[128:]
        if s > 0:
            kv_rights[s - 1].wait_recv()
            right_key = right_key + rrecv_r[s - 1, 0].astype(F32)
            right_value = right_value + rrecv_r[s - 1, 1].astype(F32)
        rsend_r[s, 0] = right_key.astype(BF16)
        rsend_r[s, 1] = right_value.astype(BF16)
        kv_rights[s].start()
        pending.append(kv_rights[s])
        if s < 3:
            if s > 0:
                kv_lefts[s - 1].wait_recv()
                left_key = left_key + rrecv_l[s - 1, 0].astype(F32)
                left_value = left_value + rrecv_l[s - 1, 1].astype(F32)
            rsend_l[s, 0] = left_key.astype(BF16)
            rsend_l[s, 1] = left_value.astype(BF16)
            kv_lefts[s].start()
            pending.append(kv_lefts[s])
            weight_step(s + 1)
        else:
            own_key, own_value = left_key, left_value

    dq_sem = sems.take(4)
    dq_copies = []
    for r in (1, 2, 3, 0):
        lanes = slice(r * 256, r * 256 + 256)
        part = nn(kt[...], dsb[:, lanes]) * SCALE
        if r == 0:
            dqown[...] = part
        else:
            k = 4 - r
            dqsend[r] = part.astype(BF16)
            dq_copies.append(
                sems.copy(dqsend.at[r], dqbuf.at[k], dq_sem + k, dq_sem + k, *group_peer(k))
            )
            dq_copies[-1].start()
    pending += dq_copies

    kv_rights[3].wait_recv()
    kv_lefts[2].wait_recv()
    totals = []
    for i, own in ((0, own_key), (1, own_value)):
        total = own + rrecv_r[3, i].astype(F32) + rrecv_l[2, i].astype(F32)
        kvfin_send[i] = total.T.astype(BF16)
    fin_send = sems.take(4)
    fin_recv = sems.take(4)
    source = lax.rem(yhi - m + 4, 4)
    fin_copies = []
    for k in range(4):
        column = lax.rem(m + k, 4)
        fin_copies.append(
            sems.copy(
                kvfin_send.at[:, pl.ds(pl.multiple_of(column * 32, 32), 32), :],
                kvfin.at[source],
                fin_send + k,
                fin_recv + source,
                g * 4 + column,
                m * 8 + z,
            )
        )
    for k in range(1, 4):
        fin_copies[k].start()
        pending.append(fin_copies[k])

    @pl.when(m != yhi)
    def _():
        fin_copies[0].start()

    @pl.when(m == yhi)
    def _():
        kvfin[0] = kvfin_send[:, pl.ds(pl.multiple_of(m * 32, 32), 32), :]

    dw_rights[3].wait_recv()
    dw_lefts[2].wait_recv()
    total = weight_block(7) + wrecv_r[3].astype(F32) + wrecv_l[2].astype(F32)
    total = total.astype(BF16)
    for y in range(4):
        dwsend[y] = total[y * 80 : y * 80 + 80, :]
    dwf_sem = sems.take(4)
    dwf_copies = []
    for k in range(1, 4):
        dwf_copies.append(
            sems.copy(
                dwsend.at[lax.rem(yhi + k, 4)], dwfin.at[yhi], dwf_sem + k, dwf_sem + k, *y_peer(k)
            )
        )
        dwf_copies[-1].start()
    pending += dwf_copies
    dwfin[yhi] = dwsend[yhi]

    for copy in dq_copies:
        copy.wait_recv()
    query_grad = dqown[...]
    for k in range(1, 4):
        query_grad = query_grad + dqbuf[k].astype(F32)
    query_rows = jnp.concatenate([query_grad[:, :128], query_grad[:, 128:]], axis=0)
    dq_ref[...] = query_rows.T.astype(BF16)

    def fin_wait(s):
        sems.copy(
            kvfin_send.at[:, pl.ds(0, 32), :],
            kvfin.at[s],
            fin_send,
            fin_recv + s,
            *y_peer(1),
        ).wait_recv()

    for s in range(1, 4):
        fin_wait(s)

    @pl.when(m != yhi)
    def _():
        fin_wait(0)

    for i, out in ((0, dk_ref), (1, dv_ref)):
        total = kvfin[0, i].astype(F32)
        for s in range(1, 4):
            total = total + kvfin[s, i].astype(F32)
        square = jnp.concatenate([total, jnp.zeros((96, 128), F32)], axis=0).T
        out[...] = square[:, :32].astype(BF16)

    for copy in dwf_copies:
        copy.wait_recv()
    columns = []
    blocks = [dwfin[q].astype(F32) for q in range(4)]
    for lo in range(2):
        for q in range(4):
            for j in range(5):
                row = (lo * 5 + j) * 8
                columns.append(blocks[q][row : row + 8, :])
    dw_ref[...] = jnp.concatenate(columns, axis=1).astype(BF16)

    for copy in pending:
        copy.wait_send()

    @pl.when(m == yhi)
    def _():
        for copy in kv_hop_copies:
            copy.wait_send()

    @pl.when(x != yhi)
    def _():
        turn_copy.wait_send()

    @pl.when(m != yhi)
    def _():
        fin_copies[0].wait_send()

    assert sems.used <= SEM_COUNT, sems.used


def per_device(block_order, query_states, key_states, value_states, out_weight, out_grad):
    v = pltpu.VMEM
    vmem = pl.BlockSpec(memory_space=pltpu.VMEM)
    scratch = [
        v((2, 128, 128), BF16),
        v((8, 2, 128, 128), BF16),
        v((4, 128, 256), BF16),
        v((1024, 128), BF16),
        v((1024, 128), BF16),
        v((1024, 128), BF16),
        v((128, 1024), BF16),
        v((128, 1024), BF16),
        v((4, 80, 128), BF16),
        v((8, 4, 80, 128), BF16),
        v((256, 1280), F32),
        v((320, 128), BF16),
        v((1280, 512), BF16),
        v((1024, 1024), F32),
        v((8, 1024), F32),
        v((1024, 1024), BF16),
        v((1024, 1024), BF16),
        v((1, 1024), F32),
        v((4, 128, 256), BF16),
        v((4, 128, 256), BF16),
        v((4, 8, 256), F32),
        v((4, 8, 256), F32),
        v((256, 512), BF16),
        v((256, 512), F32),
        v((4, 256, 128), BF16),
        v((4, 256, 128), BF16),
        v((256, 128), BF16),
        v((4, 256, 128), BF16),
        v((8, 256), F32),
        v((4, 8, 256), F32),
        v((128, 1024), BF16),
        v((1, 1024), F32),
        v((1, 1024), F32),
        v((256, 1024), BF16),
        v((4, 2, 128, 128), BF16),
        v((3, 2, 128, 128), BF16),
        v((4, 2, 128, 128), BF16),
        v((3, 2, 128, 128), BF16),
        v((2, 128, 128), BF16),
        v((4, 2, 32, 128), BF16),
        v((4, 128, 256), BF16),
        v((4, 128, 256), BF16),
        v((128, 256), F32),
        v((256, 1280), F32),
        v((4, 320, 128), BF16),
        v((3, 320, 128), BF16),
        v((4, 320, 128), BF16),
        v((3, 320, 128), BF16),
        v((4, 80, 128), BF16),
        v((4, 80, 128), BF16),
        pltpu.SemaphoreType.DMA((SEM_COUNT,)),
        pltpu.SemaphoreType.DMA((SEM_COUNT,)),
    ]
    return pl.pallas_call(
        kernel,
        out_shape=(
            jax.ShapeDtypeStruct((128, 256), BF16),
            jax.ShapeDtypeStruct((128, 256), BF16),
            jax.ShapeDtypeStruct((128, 32), BF16),
            jax.ShapeDtypeStruct((128, 32), BF16),
            jax.ShapeDtypeStruct((8, 5120), BF16),
        ),
        in_specs=[pl.BlockSpec(memory_space=pltpu.SMEM)] + [vmem] * 5,
        out_specs=[vmem] * 5,
        scratch_shapes=scratch,
        compiler_params=pltpu.CompilerParams(
            collective_id=0, has_side_effects=True, vmem_limit_bytes=48 * 1024 * 1024
        ),
        cost_estimate=pl.CostEstimate(
            flops=2_500_000_000, bytes_accessed=1_000_000, transcendentals=1_100_000
        ),
    )(block_order, query_states, key_states, value_states, out_weight, out_grad)


def solution(mesh):
    in_specs = (
        P(),
        P("ctx", "node"),
        P("ctx", None),
        P("ctx", None),
        P(("node", "ctx"), None),
        P("ctx", "node"),
    )
    out_specs = (
        P("ctx", "node"),
        P("ctx", "node"),
        P("ctx", "node"),
        P("ctx", "node"),
        P(("node", "ctx"), None),
    )
    return jax.shard_map(
        per_device, mesh=mesh, in_specs=in_specs, out_specs=out_specs, check_vma=False
    )
```

time: 885 us -> 89.7 us (0.10)
  the two profiles are of different devices: /device:TPU:6 before, /device:TPU:8 now
where the time goes in v1:
time: 89.7 us; the launch traced here: 89.4 us
  Pallas kernels  81.8 us (91%)
  local copies, waits for them, and re-layouts  6.92 us (8%)
    pallas_call x1, Pallas kernels, per_device(): pl.pallas_call(kernel, out_shape=(jax.ShapeDtypeStruct((128, 256), BF16),...  81.8 us
    unnamed x14, local copies, waits for them, and re-layouts  5.56 us

profile of v1, /device:TPU:8, one launch (start us, length us, event | category | flops | bytes accessed | tf_op | source)
XLA Modules:
  0.0 89.4 jit_solution(15917907045746678731)
XLA Ops:
  0.6 0.0 copy-start
  0.6 0.0 copy-start.4
  0.7 1.0 %copy.11.og_ref = bf16[128,320]{1,0:T(8,128)(2,1)S(1)} copy(bf16[128,320]{0,1:T(8,128)(2,1)} %param.11) | data formatting | bytes 163840 | tf_op args[5]
  1.7 0.0 copy-done
  1.7 0.0 copy-done.4
  1.7 0.0 copy-start.1
  1.7 0.9 %copy-done.1 = bf16[128,512]{1,0:T(8,128)(2,1)S(1)} copy-done((bf16[128,512]{1,0:T(8,128)(2,1)S(1)}, bf16[128,512]{1,0:T(8,128)(2,1)}, u32[]{:S(2)}) %copy-start.1) | copy-done | bytes 131096
  2.6 0.0 copy-start.2
  2.6 0.9 copy-done.2
  3.5 0.0 copy-start.3
  3.5 0.8 copy-done.3
  4.3 81.8 %shard_map.101 = (bf16[128,256]{1,0:T(8,128)(2,1)S(1)}, bf16[128,256]{1,0:T(8,128)(2,1)S(1)}, bf16[128,32]{1,0:T(8,128)(2,1)S(1)}, bf16[128,32]{1,0:T(8,128)(2,1)S(1)}, bf16[8,5120]{1,0:T(8,128)(2,1)S(1)}) custom-call(s32[64]{0:T(128)S(1)} %copy-done.4, bf16[128,256]{1,0:T(8,128)(2,1)S(1)} %copy-done.3, bf16[128,512]{1,0:T(8,128)(2,1)S(1)} %copy-done, ...), custom_call_target="tpu_custom_call" | custom-call | flops 2500000000 | bytes 1000000 | tf_op jit(solution)/shard_map/pallas_call | solution.py:741
  86.2 0.7 copy.12
  86.9 0.7 copy.13
  87.5 0.6 copy.17
  88.2 0.6 copy.18
  88.8 0.6 copy.19
Async XLA Ops:
  0.6 1.1 %copy-start = (bf16[128,512]{1,0:T(8,128)(2,1)S(1)}, bf16[128,512]{1,0:T(8,128)(2,1)}, u32[]{:S(2)}) copy-start(bf16[128,512]{1,0:T(8,128)(2,1)} %k_ref.1) | copy-start | bytes 393220
  0.6 1.1 %copy-start.4 = (s32[64]{0:T(128)S(1)}, s32[64]{0:T(128)}, u32[]{:S(2)}) copy-start(s32[64]{0:T(128)} %order_ref.1) | copy-start | bytes 772
  1.7 0.9 %copy-start.1 = (bf16[128,512]{1,0:T(8,128)(2,1)S(1)}, bf16[128,512]{1,0:T(8,128)(2,1)}, u32[]{:S(2)}) copy-start(bf16[128,512]{1,0:T(8,128)(2,1)} %v_ref.1) | copy-start | bytes 393220
  2.6 0.9 copy-start.2
  3.5 0.8 copy-start.3

commit v2 on v1

--- a/solution.py
+++ b/solution.py
@@ -54,21 +54,21 @@
         )
 
 
-SEM_COUNT = 96
+SEM_COUNT = 128
 
 
 def kernel(
     order_ref, q_ref, k_ref, v_ref, w_ref, og_ref,
     attn_ref, dq_ref, dk_ref, dv_ref, dw_ref,
-    kvg, kv, qbuf, qall, krel, vrel, kt, vt,
+    wv, kvg, kv, qbuf, qall, krel, vrel, kt, vt,
     wsl, wring, w32, ogt, dot2,
     sp, mx, pb, dsb, mloc,
     osend, obuf, ostat, ostatbuf,
-    at, gpart, gpsend, gpbuf, gown, gbuf, gstat, gstatbuf, gtall, frow, drow,
+    at, gpart, gpsend, gpfar, gpnear, gown, gbuf, gstat, gstatbuf, gtall, frow, drow,
     smp, rsend_r, rsend_l, rrecv_r, rrecv_l, kvfin_send, kvfin,
     dqsend, dqbuf, dqown,
     dwp, wsend_r, wsend_l, wrecv_r, wrecv_l, dwsend, dwfin,
-    send_sem, recv_sem,
+    send_sem, recv_sem, load_sem,
 ):
     node = lax.axis_index("node")
     ctx = lax.axis_index("ctx")
@@ -76,6 +76,8 @@
     x = lax.rem(node // 2, 4)
     ylo = node // 8
     g = node // 4
+    quarter = ylo * 2 + core
+    key_quarter = core * 2 + lax.rem(x, 2)
     m = lax.rem(node, 4)
     yhi = ctx // 8
     z = lax.rem(ctx, 8)
@@ -95,7 +97,18 @@
     x_left = ((ylo * 4 + lax.rem(x + 3, 4)) * 2 + core, ctx)
     y_flip = (((1 - ylo) * 4 + x) * 2 + core, ctx)
     sibling = (node + 1 - 2 * core, ctx)
-    turned = ((ylo * 4 + yhi) * 2 + core, x * 8 + z)
+    turned = (((yhi // 2) * 4 + x) * 2 + lax.rem(yhi, 2), quarter * 8 + z)
+
+    glane = pl.ds(pl.multiple_of(g * HD, HD), HD)
+    loads = [
+        pltpu.make_async_copy(og_ref, ogt, load_sem.at[0]),
+        pltpu.make_async_copy(w_ref, wv, load_sem.at[1]),
+        pltpu.make_async_copy(k_ref.at[:, glane], kvg.at[0], load_sem.at[2]),
+        pltpu.make_async_copy(v_ref.at[:, glane], kvg.at[1], load_sem.at[3]),
+        pltpu.make_async_copy(q_ref, qbuf.at[0], load_sem.at[4]),
+    ]
+    for load in loads:
+        load.start()
 
     barrier = pltpu.get_barrier_semaphore()
 
@@ -110,33 +123,42 @@
     for peer in (z_right, z_left, x_right, x_left, y_flip):
         greet(peer)
 
-    @pl.when(x != yhi)
+    @pl.when(quarter != yhi)
     def _():
         greet(turned)
 
-    @pl.when(m != yhi)
+    @pl.when(key_quarter != yhi)
     def _():
         for k in range(1, 4):
-            greet((g * 4 + yhi, lax.rem(yhi + k, 4) * 8 + z))
-
-    glane = pl.ds(pl.multiple_of(g * HD, HD), HD)
-    kvg[0] = k_ref[:, glane]
-    kvg[1] = v_ref[:, glane]
-    w_rows = w_ref[...].astype(F32)
-    for q in range(4):
-        slabs = []
-        for j in range(10):
-            col = 2560 * (j // 5) + 640 * q + 128 * (j % 5)
-            slabs.append(w_rows[:, col : col + 128])
-        wsl[q] = jnp.concatenate(slabs, axis=0).astype(BF16)
-    eye = (
-        lax.broadcasted_iota(jnp.int32, (320, 320), 0)
-        == lax.broadcasted_iota(jnp.int32, (320, 320), 1)
-    ).astype(F32).astype(BF16)
-    ogt[...] = nt(eye, og_ref[...]).astype(BF16)
+            greet((g * 4 + lax.rem(yhi, 2) * 2 + yhi // 2, lax.rem(yhi + k, 4) * 8 + z))
+
+    loads[0].wait()
+    low_half = lax.broadcasted_iota(jnp.int32, (8, 128), 1) < 64
+
+    def join(a, b):
+        return jnp.where(low_half, a, b)
+
+    def turn(a):
+        return pltpu.roll(a, 64, 1)
+
+    loads[1].wait()
+    w_rows = wv[...].astype(F32)
+    for half in range(2):
+        even, odd = [], []
+        for pair in range(2):
+            base = 20 * half + 10 * pair
+            w = [w_rows[:, t * 128 : t * 128 + 128] for t in range(base, base + 10)]
+            r = {t: turn(w[t]) for t in range(2, 8)}
+            shifted = {t: join(r[t], r[t + 1]) for t in range(2, 7)}
+            even += [w[0], w[1], join(w[2], shifted[4]), shifted[5], shifted[6]]
+            odd += [shifted[2], shifted[3], join(shifted[4], w[7]), w[8], w[9]]
+        wsl[2 * half] = jnp.concatenate(even, axis=0).astype(BF16)
+        wsl[2 * half + 1] = jnp.concatenate(odd, axis=0).astype(BF16)
+    for load in loads[2:]:
+        load.wait()
 
     pl.semaphore_wait(
-        barrier, 11 + jnp.where(x != yhi, 1, 0) + jnp.where(m != yhi, 3, 0)
+        barrier, 11 + jnp.where(quarter != yhi, 1, 0) + jnp.where(key_quarter != yhi, 3, 0)
     )
 
     kv_hop = sems.take(4)
@@ -144,37 +166,29 @@
         sems.copy(kvg, kv.at[7], kv_hop + k, kv_hop, *y_peer(k)) for k in range(1, 4)
     ]
 
-    @pl.when(m == yhi)
+    @pl.when(key_quarter == yhi)
     def _():
         for copy in kv_hop_copies:
             copy.start()
 
-    q_sem = sems.take(4)
-    q_copies = [
-        sems.copy(q_ref, qbuf.at[k], q_sem + k, q_sem + k, *group_peer(k)) for k in range(1, 4)
-    ]
-    for copy in q_copies:
-        copy.start()
-    pending += q_copies
-
-    def dot_rows(lo, co):
-        return pl.ds(pl.multiple_of((lo * 2 + co) * 320, 64), 320)
+    def dot_rows(position):
+        return pl.ds(pl.multiple_of(position * 320, 64), 320)
 
     def dot_lanes(position):
         return pl.ds(pl.multiple_of(position * TOK, TOK), TOK)
 
     turn_sem = sems.take(1)
     turn_copy = sems.copy(
-        ogt, dot2.at[dot_rows(ylo, core), dot_lanes(yhi)], turn_sem, turn_sem, *turned
+        ogt, dot2.at[dot_rows(x), dot_lanes(yhi)], turn_sem, turn_sem, *turned
     )
 
-    @pl.when(x != yhi)
+    @pl.when(quarter != yhi)
     def _():
         turn_copy.start()
 
-    @pl.when(x == yhi)
-    def _():
-        dot2[dot_rows(ylo, core), dot_lanes(yhi)] = ogt[...]
+    @pl.when(quarter == yhi)
+    def _():
+        dot2[dot_rows(x), dot_lanes(yhi)] = ogt[...]
 
     w_sem = sems.take(4)
     w_copies = []
@@ -189,12 +203,21 @@
     pending += w_copies
     wring[7, yhi] = wsl[yhi]
 
-    def ring(buffer):
+    q_sem = sems.take(4)
+    q_copies = [
+        sems.copy(qbuf.at[0], qbuf.at[k], q_sem + k, q_sem + k, *group_peer(k))
+        for k in range(1, 4)
+    ]
+    for copy in q_copies:
+        copy.start()
+    pending += q_copies
+
+    def ring(view):
         base = sems.take(7)
         rights = [
             sems.copy(
-                buffer.at[7 if s == 0 else RIGHT_SLOT[s - 1]],
-                buffer.at[RIGHT_SLOT[s]],
+                view(7 if s == 0 else RIGHT_SLOT[s - 1]),
+                view(RIGHT_SLOT[s]),
                 base + s,
                 base + s,
                 *z_right,
@@ -203,8 +226,8 @@
         ]
         lefts = [
             sems.copy(
-                buffer.at[7 if s == 0 else LEFT_SLOT[s - 1]],
-                buffer.at[LEFT_SLOT[s]],
+                view(7 if s == 0 else LEFT_SLOT[s - 1]),
+                view(LEFT_SLOT[s]),
                 base + 4 + s,
                 base + 4 + s,
                 *z_left,
@@ -214,46 +237,67 @@
         return rights, lefts
 
     def ring_step(rings, s):
-        rights, lefts = rings
-        if s > 0:
-            rights[s - 1].wait_recv()
+        for rights, lefts in rings:
+            if s > 0:
+                rights[s - 1].wait_recv()
             if s < 4:
+                rights[s].start()
+                pending.append(rights[s])
+            if 0 < s < 4:
                 lefts[s - 1].wait_recv()
-        if s < 4:
-            rights[s].start()
-            pending.append(rights[s])
-        if s < 3:
-            lefts[s].start()
-            pending.append(lefts[s])
-
-    kv_ring = ring(kv)
-    w_ring = ring(wring)
-
-    @pl.when(m == yhi)
+            if s < 3:
+                lefts[s].start()
+                pending.append(lefts[s])
+
+    kv_ring = [ring(lambda slot, i=i: kv.at[slot, i]) for i in range(2)]
+    w_ring = [ring(lambda slot, i=i: wring.at[slot, pl.ds(2 * i, 2)]) for i in range(2)]
+
+    @pl.when(key_quarter == yhi)
     def _():
         kv[7] = kvg[...]
 
-    @pl.when(m != yhi)
+    @pl.when(key_quarter != yhi)
     def _():
         sems.copy(kvg, kv.at[7], kv_hop, kv_hop, *y_peer(1)).wait_recv()
 
     ring_step(kv_ring, 0)
-
-    @pl.when(x != yhi)
-    def _():
-        turn_copy.wait_recv()
-
-    flip_sem = sems.take(1)
-    own_block = dot2.at[dot_rows(ylo, core), dot_lanes(x)]
-    flip_copy = sems.copy(own_block, own_block, flip_sem, flip_sem, *y_flip)
-    flip_copy.start()
-    pending.append(flip_copy)
 
     for copy in w_copies:
         copy.wait_recv()
     ring_step(w_ring, 0)
 
-    qbuf[0] = q_ref[...]
+    @pl.when(quarter != yhi)
+    def _():
+        turn_copy.wait_recv()
+
+    other_quarter = (1 - ylo) * 2 + core
+    flip_sem = sems.take(1)
+    own_block = dot2.at[dot_rows(x), dot_lanes(quarter)]
+    flip_block = dot2.at[dot_rows(x), dot_lanes(other_quarter)]
+    x_sem = sems.take(6)
+    flip_copy = sems.copy(own_block, own_block, flip_sem, flip_sem, *y_flip)
+    x_own = [
+        sems.copy(own_block, own_block, x_sem, x_sem, *x_right),
+        sems.copy(own_block, own_block, x_sem + 1, x_sem + 1, *x_left),
+    ]
+    x_flip = [
+        sems.copy(flip_block, flip_block, x_sem + 2, x_sem + 2, *x_right),
+        sems.copy(flip_block, flip_block, x_sem + 3, x_sem + 3, *x_left),
+    ]
+    for copy in [flip_copy] + x_own:
+        copy.start()
+        pending.append(copy)
+
+    def unpack_weight(slot):
+        first = lax.rem(z + OFFSET[slot], 8) * 8
+        for y in range(4):
+            block = wring[slot, y].astype(F32)
+            rows = pl.ds(pl.multiple_of(first + y * 64, 8), 8)
+            for j in range(10):
+                w32[rows, j * 128 : j * 128 + 128] = block[j * 8 : j * 8 + 8, :]
+
+    unpack_weight(7)
+
     for copy in q_copies:
         copy.wait_recv()
     for r in range(4):
@@ -272,7 +316,7 @@
     mx[...] = jnp.full(mx.shape, NEG, F32)
 
     def score_block(slot):
-        block = m * 8 + lax.rem(z + OFFSET[slot], 8)
+        block = key_quarter * 8 + lax.rem(z + OFFSET[slot], 8)
         allowed = place(block * 2, 0) <= query_place
         allowed = jnp.concatenate([allowed, allowed], axis=1)
         rows = slice(slot * 128, slot * 128 + 128)
@@ -291,50 +335,50 @@
 
     score_block(7)
 
+    flip_copy.wait_recv()
+    for copy in x_flip:
+        copy.start()
+    pending += x_flip
     ring_step(kv_ring, 1)
-    flip_copy.wait_recv()
-    x_sem = sems.take(6)
-    x_first = []
-    for lo in range(2):
-        block = dot2.at[dot_rows(lo, core), dot_lanes(x)]
-        x_first.append(sems.copy(block, block, x_sem + lo, x_sem + lo, *x_right))
-        x_first.append(sems.copy(block, block, x_sem + 2 + lo, x_sem + 2 + lo, *x_left))
-    for copy in x_first:
-        copy.start()
-    pending += x_first
+    ring_step(w_ring, 1)
     score_block(5)
     score_block(6)
-    ring_step(w_ring, 1)
-
+    unpack_weight(5)
+    unpack_weight(6)
+
+    x_own[0].wait_recv()
+    far_own = dot2.at[dot_rows(lax.rem(x + 3, 4)), dot_lanes(quarter)]
+    x_far = [sems.copy(far_own, far_own, x_sem + 4, x_sem + 4, *x_right)]
+    x_far[0].start()
+    x_own[1].wait_recv()
     ring_step(kv_ring, 2)
+    ring_step(w_ring, 2)
     score_block(3)
     score_block(4)
-    for copy in x_first:
-        copy.wait_recv()
-    from_left = dot2.at[dot_rows(0, core), dot_lanes(lax.rem(x + 3, 4))]
-    from_right = dot2.at[dot_rows(1, core), dot_lanes(lax.rem(x + 1, 4))]
-    x_second = [
-        sems.copy(from_left, from_left, x_sem + 4, x_sem + 4, *x_right),
-        sems.copy(from_right, from_right, x_sem + 5, x_sem + 5, *x_left),
-    ]
-    for copy in x_second:
-        copy.start()
-    pending += x_second
-    ring_step(w_ring, 2)
+    unpack_weight(3)
+    unpack_weight(4)
+    x_flip[1].wait_recv()
+    far_flip = dot2.at[dot_rows(lax.rem(x + 1, 4)), dot_lanes(other_quarter)]
+    x_far.append(sems.copy(far_flip, far_flip, x_sem + 5, x_sem + 5, *x_left))
+    x_far[1].start()
+    x_flip[0].wait_recv()
+    pending += x_far
 
     ring_step(kv_ring, 3)
+    ring_step(w_ring, 3)
     score_block(1)
     score_block(2)
-    for copy in x_second:
+    unpack_weight(1)
+    unpack_weight(2)
+    for copy in x_far:
         copy.wait_recv()
     core_sem = sems.take(2)
     core_copies = []
-    for lo in range(2):
-        half = dot2.at[dot_rows(lo, core), :]
-        core_copies.append(sems.copy(half, half, core_sem + lo, core_sem + lo, *sibling))
+    for i, position in enumerate((quarter, other_quarter)):
+        half = dot2.at[:, dot_lanes(position)]
+        core_copies.append(sems.copy(half, half, core_sem + i, core_sem + i, *sibling))
         core_copies[-1].start()
     pending += core_copies
-    ring_step(w_ring, 3)
 
     ring_step(kv_ring, 4)
     score_block(0)
@@ -362,7 +406,7 @@
         index = lax.broadcasted_iota(jnp.int32, (8, 256), 0)
         return jnp.where(index == 0, first, second)
 
-    for r in (1, 2, 3):
+    for r in (2, 1, 3):
         row_max, row_sum, part = forward(r)
         osend[r] = part.astype(BF16)
         ostat[r] = stat_rows(row_max, row_sum)
@@ -375,36 +419,54 @@
         o_copies[-2].start()
         o_copies[-1].start()
     pending += o_copies
-    own_max, own_sum, own_part = forward(0)
-    obuf_own = own_part
-
     ring_step(w_ring, 4)
-    for slot in range(8):
-        first = lax.rem(z + OFFSET[slot], 8) * 8
-        for y in range(4):
-            block = wring[slot, y].astype(F32)
-            rows = pl.ds(pl.multiple_of(first + y * 64, 8), 8)
-            for j in range(10):
-                w32[rows, j * 128 : j * 128 + 128] = block[j * 8 : j * 8 + 8, :]
+    unpack_weight(0)
+    weight = w32[...].astype(BF16)
     for copy in core_copies:
         copy.wait_recv()
-    weight = w32[...].astype(BF16)
     gpart[...] = nn(weight, dot2[...])
-    gp_sem = sems.take(4)
-    gp_copies = []
-    for k in range(1, 4):
-        gpsend[k] = gpart[:, dot_lanes(lax.rem(yhi + k, 4))].astype(BF16)
-        gp_copies.append(
-            sems.copy(gpsend.at[k], gpbuf.at[k], gp_sem + k, gp_sem + k, *y_peer(k))
-        )
-        gp_copies[-1].start()
-    pending += gp_copies
+    heads = (slice(0, 128), slice(128, 256))
+    lanes_of = [dot_lanes(lax.rem(yhi + k, 4)) for k in range(4)]
+    gp_sem = sems.take(6)
+    gp_far, gp_direct, gp_through = [], [], []
+    for way, k in ((0, 1), (1, 3)):
+        gpsend[way] = gpart[heads[way], lanes_of[2]].astype(BF16)
+        gp_far.append(
+            sems.copy(gpsend.at[way], gpfar.at[way], gp_sem + way, gp_sem + way, *y_peer(k))
+        )
+        gp_far[way].start()
+    for way, k in ((0, 1), (1, 3)):
+        gpsend[2 + way] = gpart[heads[1 - way], lanes_of[k]].astype(BF16)
+        gp_direct.append(
+            sems.copy(
+                gpsend.at[2 + way], gpnear.at[way], gp_sem + 2 + way, gp_sem + 2 + way, *y_peer(k)
+            )
+        )
+        gp_direct[way].start()
+    pending += gp_far + gp_direct
+    own_max, own_sum, own_part = forward(0)
+    for way, k in ((0, 1), (1, 3)):
+        gp_far[way].wait_recv()
+        gpsend[4 + way] = (
+            gpart[heads[way], lanes_of[k]] + gpfar[way].astype(F32)
+        ).astype(BF16)
+        gp_through.append(
+            sems.copy(
+                gpsend.at[4 + way],
+                gpnear.at[2 + way],
+                gp_sem + 4 + way,
+                gp_sem + 4 + way,
+                *y_peer(k),
+            )
+        )
+        gp_through[way].start()
+    pending += gp_through
 
     for copy in o_copies:
         copy.wait_recv()
     maxes = [own_max] + [ostatbuf[k, 0:1, :] for k in range(1, 4)]
     sums = [own_sum] + [ostatbuf[k, 1:2, :] for k in range(1, 4)]
-    parts = [obuf_own] + [obuf[k].astype(F32) for k in range(1, 4)]
+    parts = [own_part] + [obuf[k].astype(F32) for k in range(1, 4)]
     top = functools.reduce(jnp.maximum, maxes)
     factors = [jnp.exp2(value - top) for value in maxes]
     total = sum(f * s for f, s in zip(factors, sums))
@@ -412,22 +474,28 @@
     lse = top + jnp.log2(total)
     attention_rows = jnp.concatenate([attention[:, :128], attention[:, 128:]], axis=0)
     attention_bf = attention_rows.astype(BF16)
-    my_lanes = dot_lanes(yhi)
+    my_lanes = lanes_of[0]
     at[:, my_lanes] = attention_bf
-    at_sem = sems.take(4)
+    at_sem = sems.take(6)
     at_copies = []
-    for k in range(1, 4):
-        mine = at.at[:, my_lanes]
-        at_copies.append(sems.copy(mine, mine, at_sem + k, at_sem + k, *y_peer(k)))
-        at_copies[-1].start()
+    for way, k in ((0, 1), (1, 3)):
+        for i, head in enumerate((way, 1 - way)):
+            mine = at.at[heads[head], my_lanes]
+            sem = at_sem + way * 2 + i
+            at_copies.append(sems.copy(mine, mine, sem, sem, *y_peer(k)))
+            at_copies[-1].start()
     pending += at_copies
     attn_ref[...] = attention_rows.T.astype(BF16)
 
-    for copy in gp_copies:
+    for copy in gp_direct + gp_through:
         copy.wait_recv()
-    grad = gpart[:, my_lanes]
-    for k in range(1, 4):
-        grad = grad + gpbuf[k].astype(F32)
+    grad = gpart[:, my_lanes] + jnp.concatenate(
+        [
+            gpnear[1].astype(F32) + gpnear[2].astype(F32),
+            gpnear[0].astype(F32) + gpnear[3].astype(F32),
+        ],
+        axis=0,
+    )
     grad_bf = grad.astype(BF16)
     gown[...] = grad_bf
     products = grad_bf.astype(F32) * attention_bf.astype(F32)
@@ -452,14 +520,18 @@
         g_copies[-1].start()
     pending += g_copies
 
-    for copy in at_copies:
-        copy.wait_recv()
-    dwp[...] = nt(at[...], dot2[...])
-
-    def weight_block(slot):
+    at_far = []
+    for way, k in ((0, 1), (1, 3)):
+        at_copies[2 * way].wait_recv()
+        passed = at.at[heads[way], lanes_of[4 - k]]
+        at_far.append(sems.copy(passed, passed, at_sem + 4 + way, at_sem + 4 + way, *y_peer(k)))
+        at_far[way].start()
+    pending += at_far
+
+    def weight_block(slot, part):
         first = lax.rem(z + OFFSET[slot], 8) * 8
         slabs = []
-        for y in range(4):
+        for y in (2 * part, 2 * part + 1):
             rows = pl.ds(pl.multiple_of(first + y * 64, 8), 8)
             for j in range(10):
                 slabs.append(dwp[rows, j * 128 : j * 128 + 128])
@@ -477,26 +549,27 @@
         ]
         return rights, lefts
 
-    dw_rights, dw_lefts = sum_ring(wsend_r, wrecv_r, wsend_l, wrecv_l)
+    dw_rings = [
+        sum_ring(wsend_r.at[i], wrecv_r.at[i], wsend_l.at[i], wrecv_l.at[i]) for i in range(2)
+    ]
 
     def weight_step(s):
-        right = weight_block(2 * s)
-        if s > 0:
-            dw_rights[s - 1].wait_recv()
-            right = right + wrecv_r[s - 1].astype(F32)
-        wsend_r[s] = right.astype(BF16)
-        dw_rights[s].start()
-        pending.append(dw_rights[s])
-        if s < 3:
-            left = weight_block(2 * s + 1)
+        for i, (rights, lefts) in enumerate(dw_rings):
+            right = weight_block(2 * s, i)
             if s > 0:
-                dw_lefts[s - 1].wait_recv()
-                left = left + wrecv_l[s - 1].astype(F32)
-            wsend_l[s] = left.astype(BF16)
-            dw_lefts[s].start()
-            pending.append(dw_lefts[s])
-
-    weight_step(0)
+                rights[s - 1].wait_recv()
+                right = right + wrecv_r[i, s - 1].astype(F32)
+            wsend_r[i, s] = right.astype(BF16)
+            rights[s].start()
+            pending.append(rights[s])
+            if s < 3:
+                left = weight_block(2 * s + 1, i)
+                if s > 0:
+                    lefts[s - 1].wait_recv()
+                    left = left + wrecv_l[i, s - 1].astype(F32)
+                wsend_l[i, s] = left.astype(BF16)
+                lefts[s].start()
+                pending.append(lefts[s])
 
     for copy in g_copies:
         copy.wait_recv()
@@ -548,9 +621,13 @@
             rsend_l[s, 1] = left_value.astype(BF16)
             kv_lefts[s].start()
             pending.append(kv_lefts[s])
-            weight_step(s + 1)
         else:
             own_key, own_value = left_key, left_value
+        if s == 0:
+            for copy in (at_copies[1], at_copies[3], at_far[0], at_far[1]):
+                copy.wait_recv()
+            dwp[...] = nt(at[...], dot2[...])
+        weight_step(s)
 
     dq_sem = sems.take(4)
     dq_copies = []
@@ -576,7 +653,7 @@
         kvfin_send[i] = total.T.astype(BF16)
     fin_send = sems.take(4)
     fin_recv = sems.take(4)
-    source = lax.rem(yhi - m + 4, 4)
+    source = lax.rem(yhi - key_quarter + 4, 4)
     fin_copies = []
     for k in range(4):
         column = lax.rem(m + k, 4)
@@ -587,27 +664,28 @@
                 fin_send + k,
                 fin_recv + source,
                 g * 4 + column,
-                m * 8 + z,
+                key_quarter * 8 + z,
             )
         )
     for k in range(1, 4):
         fin_copies[k].start()
         pending.append(fin_copies[k])
 
-    @pl.when(m != yhi)
+    @pl.when(key_quarter != yhi)
     def _():
         fin_copies[0].start()
 
-    @pl.when(m == yhi)
+    @pl.when(key_quarter == yhi)
     def _():
         kvfin[0] = kvfin_send[:, pl.ds(pl.multiple_of(m * 32, 32), 32), :]
 
-    dw_rights[3].wait_recv()
-    dw_lefts[2].wait_recv()
-    total = weight_block(7) + wrecv_r[3].astype(F32) + wrecv_l[2].astype(F32)
-    total = total.astype(BF16)
-    for y in range(4):
-        dwsend[y] = total[y * 80 : y * 80 + 80, :]
+    for i, (rights, lefts) in enumerate(dw_rings):
+        rights[3].wait_recv()
+        lefts[2].wait_recv()
+        total = weight_block(7, i) + wrecv_r[i, 3].astype(F32) + wrecv_l[i, 2].astype(F32)
+        total = total.astype(BF16)
+        for y in range(2):
+            dwsend[2 * i + y] = total[y * 80 : y * 80 + 80, :]
     dwf_sem = sems.take(4)
     dwf_copies = []
     for k in range(1, 4):
@@ -640,7 +718,7 @@
     for s in range(1, 4):
         fin_wait(s)
 
-    @pl.when(m != yhi)
+    @pl.when(key_quarter != yhi)
     def _():
         fin_wait(0)
 
@@ -648,43 +726,76 @@
         total = kvfin[0, i].astype(F32)
         for s in range(1, 4):
             total = total + kvfin[s, i].astype(F32)
-        square = jnp.concatenate([total, jnp.zeros((96, 128), F32)], axis=0).T
-        out[...] = square[:, :32].astype(BF16)
+        out[...] = total.astype(BF16)
 
     for copy in dwf_copies:
         copy.wait_recv()
     columns = []
     blocks = [dwfin[q].astype(F32) for q in range(4)]
-    for lo in range(2):
-        for q in range(4):
-            for j in range(5):
-                row = (lo * 5 + j) * 8
-                columns.append(blocks[q][row : row + 8, :])
+    for half in range(2):
+        for pair in range(2):
+            a, c = (
+                [
+                    blocks[2 * half + i][(pair * 5 + t) * 8 : (pair * 5 + t) * 8 + 8, :]
+                    for t in range(5)
+                ]
+                for i in range(2)
+            )
+            columns += [
+                a[0],
+                a[1],
+                join(a[2], turn(c[0])),
+                join(turn(c[0]), turn(c[1])),
+                join(turn(c[1]), turn(c[2])),
+                join(turn(a[2]), turn(a[3])),
+                join(turn(a[3]), turn(a[4])),
+                join(turn(a[4]), c[2]),
+                c[3],
+                c[4],
+            ]
     dw_ref[...] = jnp.concatenate(columns, axis=1).astype(BF16)
 
     for copy in pending:
         copy.wait_send()
 
-    @pl.when(m == yhi)
+    @pl.when(key_quarter == yhi)
     def _():
         for copy in kv_hop_copies:
             copy.wait_send()
 
-    @pl.when(x != yhi)
+    @pl.when(quarter != yhi)
     def _():
         turn_copy.wait_send()
 
-    @pl.when(m != yhi)
+    @pl.when(key_quarter != yhi)
     def _():
         fin_copies[0].wait_send()
 
     assert sems.used <= SEM_COUNT, sems.used
+
+
+def deliver_kernel(*refs):
+    count = len(refs) // 2
+    for i in range(count):
+        refs[count + i][...] = refs[i][...]
+
+
+def deliver(results):
+    vmem = pl.BlockSpec(memory_space=pltpu.VMEM)
+    return pl.pallas_call(
+        deliver_kernel,
+        out_shape=[jax.ShapeDtypeStruct(r.shape, r.dtype) for r in results],
+        in_specs=[vmem] * len(results),
+        out_specs=[vmem] * len(results),
+        compiler_params=pltpu.CompilerParams(vmem_limit_bytes=63 * 1024 * 1024),
+    )(*results)
 
 
 def per_device(block_order, query_states, key_states, value_states, out_weight, out_grad):
     v = pltpu.VMEM
     vmem = pl.BlockSpec(memory_space=pltpu.VMEM)
     scratch = [
+        v((8, 5120), BF16),
         v((2, 128, 128), BF16),
         v((8, 2, 128, 128), BF16),
         v((4, 128, 256), BF16),
@@ -709,8 +820,9 @@
         v((4, 8, 256), F32),
         v((256, 512), BF16),
         v((256, 512), F32),
-        v((4, 256, 128), BF16),
-        v((4, 256, 128), BF16),
+        v((6, 128, 128), BF16),
+        v((2, 128, 128), BF16),
+        v((4, 128, 128), BF16),
         v((256, 128), BF16),
         v((4, 256, 128), BF16),
         v((8, 256), F32),
@@ -729,34 +841,37 @@
         v((4, 128, 256), BF16),
         v((128, 256), F32),
         v((256, 1280), F32),
-        v((4, 320, 128), BF16),
-        v((3, 320, 128), BF16),
-        v((4, 320, 128), BF16),
-        v((3, 320, 128), BF16),
+        v((2, 4, 160, 128), BF16),
+        v((2, 3, 160, 128), BF16),
+        v((2, 4, 160, 128), BF16),
+        v((2, 3, 160, 128), BF16),
         v((4, 80, 128), BF16),
         v((4, 80, 128), BF16),
         pltpu.SemaphoreType.DMA((SEM_COUNT,)),
         pltpu.SemaphoreType.DMA((SEM_COUNT,)),
+        pltpu.SemaphoreType.DMA((5,)),
     ]
-    return pl.pallas_call(
+    results = pl.pallas_call(
         kernel,
         out_shape=(
             jax.ShapeDtypeStruct((128, 256), BF16),
             jax.ShapeDtypeStruct((128, 256), BF16),
-            jax.ShapeDtypeStruct((128, 32), BF16),
-            jax.ShapeDtypeStruct((128, 32), BF16),
+            jax.ShapeDtypeStruct((32, 128), BF16),
+            jax.ShapeDtypeStruct((32, 128), BF16),
             jax.ShapeDtypeStruct((8, 5120), BF16),
         ),
-        in_specs=[pl.BlockSpec(memory_space=pltpu.SMEM)] + [vmem] * 5,
+        in_specs=[pl.BlockSpec(memory_space=pltpu.SMEM)] + [pl.BlockSpec(memory_space=pltpu.HBM)] * 5,
         out_specs=[vmem] * 5,
         scratch_shapes=scratch,
         compiler_params=pltpu.CompilerParams(
-            collective_id=0, has_side_effects=True, vmem_limit_bytes=48 * 1024 * 1024
+            collective_id=0, has_side_effects=True, vmem_limit_bytes=63 * 1024 * 1024
         ),
         cost_estimate=pl.CostEstimate(
             flops=2_500_000_000, bytes_accessed=1_000_000, transcendentals=1_100_000
         ),
-    )(block_order, query_states, key_states, value_states, out_weight, out_grad)
+    )(block_order, query_states, key_states, value_states, out_weight, out_grad.T)
+    results = deliver(results)
+    return results[0], results[1], results[2].T, results[3].T, results[4]
 
 
 def solution(mesh):

time: 89.7 us -> 80.9 us (0.902)
  the two profiles are of different devices: /device:TPU:8 before, /device:TPU:6 now
where the time goes in v2:
time: 80.9 us; the launch traced here: 80.2 us
  Pallas kernels  79.5 us (98%)
    pallas_call x1, Pallas kernels, per_device(): pl.pallas_call(kernel, out_shape=(jax.ShapeDtypeStruct((128, 256), BF16),...  77.8 us
    pallas_call x1, Pallas kernels, deliver(): pl.pallas_call(deliver_kernel, out_shape=[jax.ShapeDtypeStruct(r.shape, r...  1.68 us

profile of v2, /device:TPU:6, one launch (start us, length us, event | category | flops | bytes accessed | tf_op | source)
XLA Modules:
  0.0 80.2 jit_solution(4872278853994345593)
XLA Ops:
  0.6 77.8 %shard_map.101 = (bf16[128,256]{1,0:T(8,128)(2,1)}, bf16[128,256]{1,0:T(8,128)(2,1)}, bf16[32,128]{1,0:T(8,128)(2,1)}, bf16[32,128]{1,0:T(8,128)(2,1)}, bf16[8,5120]{1,0:T(8,128)(2,1)}) custom-call(s32[64]{0:T(128)} %order_ref.1, bf16[128,256]{1,0:T(8,128)(2,1)} %q_ref.1, bf16[128,512]{1,0:T(8,128)(2,1)} %k_ref.1, bf16[128,512]{1,0:T(8,128)(2,1)} %v_ref.1, ...), custom_call_target="tpu_custom_call" | custom-call | flops 2500000000 | bytes 1000000 | tf_op jit(solution)/shard_map/pallas_call | solution.py:854
  78.5 1.7 %shard_map.102 = (bf16[128,256]{1,0:T(8,128)(2,1)}, bf16[128,256]{1,0:T(8,128)(2,1)}, bf16[32,128]{1,0:T(8,128)(2,1)}, bf16[32,128]{1,0:T(8,128)(2,1)}, bf16[8,5120]{1,0:T(8,128)(2,1)}) custom-call(bf16[128,256]{1,0:T(8,128)(2,1)} %get-tuple-element.15.refs_0_, bf16[128,256]{1,0:T(8,128)(2,1)} %get-tuple-element.16.refs_1_, ...), custom_call_target="tpu_custom_call" | custom-call | tf_op jit(solution)/shard_map/pallas_call | solution.py:785

commit v3 on v2

--- a/solution.py
+++ b/solution.py
@@ -19,7 +19,10 @@
 
 OFFSET = (4, 5, 3, 6, 2, 7, 1, 0)
 RIGHT_SLOT = (5, 3, 1, 0)
-LEFT_SLOT = (6, 4, 2)
+LEFT_SLOT = (6, 4, 2, 0)
+STEPS = ((4, 3), (3, 4))
+RIGHT_SUM = ((0, 2, 4, 6), (2, 4, 6))
+LEFT_SUM = ((1, 3, 5), (0, 1, 3, 5))
 
 
 def nn(a, b):
@@ -65,9 +68,9 @@
     sp, mx, pb, dsb, mloc,
     osend, obuf, ostat, ostatbuf,
     at, gpart, gpsend, gpfar, gpnear, gown, gbuf, gstat, gstatbuf, gtall, frow, drow,
-    smp, rsend_r, rsend_l, rrecv_r, rrecv_l, kvfin_send, kvfin,
+    smp, kvpart, rsend, rrecv, kvfin_send, kvfin,
     dqsend, dqbuf, dqown,
-    dwp, wsend_r, wsend_l, wrecv_r, wrecv_l, dwsend, dwfin,
+    dwp, wsend, wrecv, dwsend, dwfin,
     send_sem, recv_sem, load_sem,
 ):
     node = lax.axis_index("node")
@@ -161,16 +164,6 @@
         barrier, 11 + jnp.where(quarter != yhi, 1, 0) + jnp.where(key_quarter != yhi, 3, 0)
     )
 
-    kv_hop = sems.take(4)
-    kv_hop_copies = [
-        sems.copy(kvg, kv.at[7], kv_hop + k, kv_hop, *y_peer(k)) for k in range(1, 4)
-    ]
-
-    @pl.when(key_quarter == yhi)
-    def _():
-        for copy in kv_hop_copies:
-            copy.start()
-
     def dot_rows(position):
         return pl.ds(pl.multiple_of(position * 320, 64), 320)
 
@@ -203,6 +196,16 @@
     pending += w_copies
     wring[7, yhi] = wsl[yhi]
 
+    kv_hop = sems.take(4)
+    kv_hop_copies = [
+        sems.copy(kvg, kv.at[7], kv_hop + k, kv_hop, *y_peer(k)) for k in range(1, 4)
+    ]
+
+    @pl.when(key_quarter == yhi)
+    def _():
+        for copy in kv_hop_copies:
+            copy.start()
+
     q_sem = sems.take(4)
     q_copies = [
         sems.copy(qbuf.at[0], qbuf.at[k], q_sem + k, q_sem + k, *group_peer(k))
@@ -212,59 +215,36 @@
         copy.start()
     pending += q_copies
 
-    def ring(view):
+    def ring(half, view):
         base = sems.take(7)
-        rights = [
-            sems.copy(
-                view(7 if s == 0 else RIGHT_SLOT[s - 1]),
-                view(RIGHT_SLOT[s]),
-                base + s,
-                base + s,
-                *z_right,
+        ways = []
+        for count, slots, peer in zip(STEPS[half], (RIGHT_SLOT, LEFT_SLOT), (z_right, z_left)):
+            ways.append(
+                [
+                    sems.copy(
+                        view(7 if s == 0 else slots[s - 1]),
+                        view(slots[s]),
+                        base + s,
+                        base + s,
+                        *peer,
+                    )
+                    for s in range(count)
+                ]
             )
-            for s in range(4)
-        ]
-        lefts = [
-            sems.copy(
-                view(7 if s == 0 else LEFT_SLOT[s - 1]),
-                view(LEFT_SLOT[s]),
-                base + 4 + s,
-                base + 4 + s,
-                *z_left,
-            )
-            for s in range(3)
-        ]
-        return rights, lefts
+            base += count
+        return ways
 
     def ring_step(rings, s):
-        for rights, lefts in rings:
-            if s > 0:
-                rights[s - 1].wait_recv()
-            if s < 4:
-                rights[s].start()
-                pending.append(rights[s])
-            if 0 < s < 4:
-                lefts[s - 1].wait_recv()
-            if s < 3:
-                lefts[s].start()
-                pending.append(lefts[s])
-
-    kv_ring = [ring(lambda slot, i=i: kv.at[slot, i]) for i in range(2)]
-    w_ring = [ring(lambda slot, i=i: wring.at[slot, pl.ds(2 * i, 2)]) for i in range(2)]
-
-    @pl.when(key_quarter == yhi)
-    def _():
-        kv[7] = kvg[...]
-
-    @pl.when(key_quarter != yhi)
-    def _():
-        sems.copy(kvg, kv.at[7], kv_hop, kv_hop, *y_peer(1)).wait_recv()
-
-    ring_step(kv_ring, 0)
-
-    for copy in w_copies:
-        copy.wait_recv()
-    ring_step(w_ring, 0)
+        for ways in rings:
+            for copies in ways:
+                if 0 < s <= len(copies):
+                    copies[s - 1].wait_recv()
+                if s < len(copies):
+                    copies[s].start()
+                    pending.append(copies[s])
+
+    kv_ring = [ring(i, lambda slot, i=i: kv.at[slot, i]) for i in range(2)]
+    w_ring = [ring(i, lambda slot, i=i: wring.at[slot, pl.ds(2 * i, 2)]) for i in range(2)]
 
     @pl.when(quarter != yhi)
     def _():
@@ -288,6 +268,32 @@
         copy.start()
         pending.append(copy)
 
+    core_sem = sems.take(8)
+    core_copies = []
+
+    def share(row_position, lane_position):
+        block = dot2.at[dot_rows(row_position), dot_lanes(lane_position)]
+        sem = core_sem + len(core_copies)
+        core_copies.append(sems.copy(block, block, sem, sem, *sibling))
+        core_copies[-1].start()
+        pending.append(core_copies[-1])
+
+    share(x, quarter)
+
+    for copy in w_copies:
+        copy.wait_recv()
+    ring_step(w_ring, 0)
+
+    @pl.when(key_quarter == yhi)
+    def _():
+        kv[7] = kvg[...]
+
+    @pl.when(key_quarter != yhi)
+    def _():
+        sems.copy(kvg, kv.at[7], kv_hop, kv_hop, *y_peer(1)).wait_recv()
+
+    ring_step(kv_ring, 0)
+
     def unpack_weight(slot):
         first = lax.rem(z + OFFSET[slot], 8) * 8
         for y in range(4):
@@ -339,8 +345,9 @@
     for copy in x_flip:
         copy.start()
     pending += x_flip
+    share(x, other_quarter)
+    ring_step(w_ring, 1)
     ring_step(kv_ring, 1)
-    ring_step(w_ring, 1)
     score_block(5)
     score_block(6)
     unpack_weight(5)
@@ -351,8 +358,10 @@
     x_far = [sems.copy(far_own, far_own, x_sem + 4, x_sem + 4, *x_right)]
     x_far[0].start()
     x_own[1].wait_recv()
+    share(lax.rem(x + 3, 4), quarter)
+    share(lax.rem(x + 1, 4), quarter)
+    ring_step(w_ring, 2)
     ring_step(kv_ring, 2)
-    ring_step(w_ring, 2)
     score_block(3)
     score_block(4)
     unpack_weight(3)
@@ -362,24 +371,47 @@
     x_far.append(sems.copy(far_flip, far_flip, x_sem + 5, x_sem + 5, *x_left))
     x_far[1].start()
     x_flip[0].wait_recv()
+    share(lax.rem(x + 3, 4), other_quarter)
+    share(lax.rem(x + 1, 4), other_quarter)
     pending += x_far
 
+    ring_step(w_ring, 3)
     ring_step(kv_ring, 3)
-    ring_step(w_ring, 3)
     score_block(1)
     score_block(2)
     unpack_weight(1)
     unpack_weight(2)
     for copy in x_far:
         copy.wait_recv()
-    core_sem = sems.take(2)
-    core_copies = []
-    for i, position in enumerate((quarter, other_quarter)):
-        half = dot2.at[:, dot_lanes(position)]
-        core_copies.append(sems.copy(half, half, core_sem + i, core_sem + i, *sibling))
-        core_copies[-1].start()
-    pending += core_copies
-
+    share(lax.rem(x + 2, 4), quarter)
+    share(lax.rem(x + 2, 4), other_quarter)
+
+    ring_step(w_ring, 4)
+    unpack_weight(0)
+    weight = w32[...].astype(BF16)
+    for copy in core_copies:
+        copy.wait_recv()
+    gpart[...] = nn(weight, dot2[...])
+    heads = (slice(0, 128), slice(128, 256))
+    lanes_of = [dot_lanes(lax.rem(yhi + k, 4)) for k in range(4)]
+    my_lanes = lanes_of[0]
+    gp_sem = sems.take(6)
+    gp_far, gp_direct, gp_through = [], [], []
+    for way, k in ((0, 1), (1, 3)):
+        gpsend[way] = gpart[heads[way], lanes_of[2]].astype(BF16)
+        gp_far.append(
+            sems.copy(gpsend.at[way], gpfar.at[way], gp_sem + way, gp_sem + way, *y_peer(k))
+        )
+        gp_far[way].start()
+    for way, k in ((0, 1), (1, 3)):
+        gpsend[2 + way] = gpart[heads[1 - way], lanes_of[k]].astype(BF16)
+        gp_direct.append(
+            sems.copy(
+                gpsend.at[2 + way], gpnear.at[way], gp_sem + 2 + way, gp_sem + 2 + way, *y_peer(k)
+            )
+        )
+        gp_direct[way].start()
+    pending += gp_far + gp_direct
     ring_step(kv_ring, 4)
     score_block(0)
 
@@ -419,32 +451,6 @@
         o_copies[-2].start()
         o_copies[-1].start()
     pending += o_copies
-    ring_step(w_ring, 4)
-    unpack_weight(0)
-    weight = w32[...].astype(BF16)
-    for copy in core_copies:
-        copy.wait_recv()
-    gpart[...] = nn(weight, dot2[...])
-    heads = (slice(0, 128), slice(128, 256))
-    lanes_of = [dot_lanes(lax.rem(yhi + k, 4)) for k in range(4)]
-    gp_sem = sems.take(6)
-    gp_far, gp_direct, gp_through = [], [], []
-    for way, k in ((0, 1), (1, 3)):
-        gpsend[way] = gpart[heads[way], lanes_of[2]].astype(BF16)
-        gp_far.append(
-            sems.copy(gpsend.at[way], gpfar.at[way], gp_sem + way, gp_sem + way, *y_peer(k))
-        )
-        gp_far[way].start()
-    for way, k in ((0, 1), (1, 3)):
-        gpsend[2 + way] = gpart[heads[1 - way], lanes_of[k]].astype(BF16)
-        gp_direct.append(
-            sems.copy(
-                gpsend.at[2 + way], gpnear.at[way], gp_sem + 2 + way, gp_sem + 2 + way, *y_peer(k)
-            )
-        )
-        gp_direct[way].start()
-    pending += gp_far + gp_direct
-    own_max, own_sum, own_part = forward(0)
     for way, k in ((0, 1), (1, 3)):
         gp_far[way].wait_recv()
         gpsend[4 + way] = (
@@ -462,6 +468,25 @@
         gp_through[way].start()
     pending += gp_through
 
+    own_max, own_sum, own_part = forward(0)
+
+    for copy in gp_direct + gp_through:
+        copy.wait_recv()
+    grad = gpart[:, my_lanes] + jnp.concatenate(
+        [
+            gpnear[1].astype(F32) + gpnear[2].astype(F32),
+            gpnear[0].astype(F32) + gpnear[3].astype(F32),
+        ],
+        axis=0,
+    )
+    grad_bf = grad.astype(BF16)
+    gown[...] = grad_bf
+    g_sem = sems.take(8)
+    g_copies = []
+    for k in range(1, 4):
+        g_copies.append(sems.copy(gown, gbuf.at[k], g_sem + k, g_sem + k, *group_peer(k)))
+        g_copies[-1].start()
+
     for copy in o_copies:
         copy.wait_recv()
     maxes = [own_max] + [ostatbuf[k, 0:1, :] for k in range(1, 4)]
@@ -474,7 +499,6 @@
     lse = top + jnp.log2(total)
     attention_rows = jnp.concatenate([attention[:, :128], attention[:, 128:]], axis=0)
     attention_bf = attention_rows.astype(BF16)
-    my_lanes = lanes_of[0]
     at[:, my_lanes] = attention_bf
     at_sem = sems.take(6)
     at_copies = []
@@ -485,19 +509,6 @@
             at_copies.append(sems.copy(mine, mine, sem, sem, *y_peer(k)))
             at_copies[-1].start()
     pending += at_copies
-    attn_ref[...] = attention_rows.T.astype(BF16)
-
-    for copy in gp_direct + gp_through:
-        copy.wait_recv()
-    grad = gpart[:, my_lanes] + jnp.concatenate(
-        [
-            gpnear[1].astype(F32) + gpnear[2].astype(F32),
-            gpnear[0].astype(F32) + gpnear[3].astype(F32),
-        ],
-        axis=0,
-    )
-    grad_bf = grad.astype(BF16)
-    gown[...] = grad_bf
     products = grad_bf.astype(F32) * attention_bf.astype(F32)
     row_dot = jnp.concatenate(
         [
@@ -508,18 +519,14 @@
     )
     own_stat = stat_rows(lse, row_dot)
     gstat[...] = own_stat
-    g_sem = sems.take(8)
-    g_copies = []
     for k in range(1, 4):
-        peer = group_peer(k)
-        g_copies.append(sems.copy(gown, gbuf.at[k], g_sem + k, g_sem + k, *peer))
         g_copies.append(
-            sems.copy(gstat, gstatbuf.at[k], g_sem + 4 + k, g_sem + 4 + k, *peer)
-        )
-        g_copies[-2].start()
+            sems.copy(gstat, gstatbuf.at[k], g_sem + 4 + k, g_sem + 4 + k, *group_peer(k))
+        )
         g_copies[-1].start()
     pending += g_copies
 
+    attn_ref[...] = attention_rows.T.astype(BF16)
     at_far = []
     for way, k in ((0, 1), (1, 3)):
         at_copies[2 * way].wait_recv()
@@ -537,39 +544,52 @@
                 slabs.append(dwp[rows, j * 128 : j * 128 + 128])
         return jnp.concatenate(slabs, axis=0)
 
-    def sum_ring(sends_r, recvs_r, sends_l, recvs_l):
+    def sum_ring(half, block, sends, recvs):
         base = sems.take(7)
-        rights = [
-            sems.copy(sends_r.at[s], recvs_r.at[s], base + s, base + s, *z_right)
-            for s in range(4)
-        ]
-        lefts = [
-            sems.copy(sends_l.at[s], recvs_l.at[s], base + 4 + s, base + 4 + s, *z_left)
-            for s in range(3)
-        ]
-        return rights, lefts
+        ways = []
+        for way, (slots, peer) in enumerate(((RIGHT_SUM, z_right), (LEFT_SUM, z_left))):
+            slots = slots[half]
+            ways.append(
+                (
+                    way,
+                    slots,
+                    [
+                        sems.copy(
+                            sends.at[half, way, s],
+                            recvs.at[half, way, s],
+                            base + s,
+                            base + s,
+                            *peer,
+                        )
+                        for s in range(len(slots))
+                    ],
+                )
+            )
+            base += len(slots)
+
+        def step(s):
+            for way, slots, copies in ways:
+                if s < len(slots):
+                    value = block(slots[s])
+                    if s > 0:
+                        copies[s - 1].wait_recv()
+                        value = value + recvs[half, way, s - 1].astype(F32)
+                    sends[half, way, s] = value.astype(BF16)
+                    copies[s].start()
+                    pending.append(copies[s])
+
+        def finish():
+            total = block(7)
+            for way, slots, copies in ways:
+                copies[-1].wait_recv()
+                total = total + recvs[half, way, len(slots) - 1].astype(F32)
+            return total
+
+        return step, finish
 
     dw_rings = [
-        sum_ring(wsend_r.at[i], wrecv_r.at[i], wsend_l.at[i], wrecv_l.at[i]) for i in range(2)
+        sum_ring(i, lambda slot, i=i: weight_block(slot, i), wsend, wrecv) for i in range(2)
     ]
-
-    def weight_step(s):
-        for i, (rights, lefts) in enumerate(dw_rings):
-            right = weight_block(2 * s, i)
-            if s > 0:
-                rights[s - 1].wait_recv()
-                right = right + wrecv_r[i, s - 1].astype(F32)
-            wsend_r[i, s] = right.astype(BF16)
-            rights[s].start()
-            pending.append(rights[s])
-            if s < 3:
-                left = weight_block(2 * s + 1, i)
-                if s > 0:
-                    lefts[s - 1].wait_recv()
-                    left = left + wrecv_l[i, s - 1].astype(F32)
-                wsend_l[i, s] = left.astype(BF16)
-                lefts[s].start()
-                pending.append(lefts[s])
 
     for copy in g_copies:
         copy.wait_recv()
@@ -584,7 +604,10 @@
         frow[:, lanes] = jnp.exp2(mloc[:, lanes] - stat[0:1, :])
         drow[:, lanes] = stat[1:2, :]
 
-    kv_rights, kv_lefts = sum_ring(rsend_r, rrecv_r, rsend_l, rrecv_l)
+    kv_sum_rings = [
+        sum_ring(i, lambda slot, i=i: kvpart[i, slot * 128 : slot * 128 + 128, :], rsend, rrecv)
+        for i in range(2)
+    ]
 
     def backward(s):
         rows = slice(s * 256, s * 256 + 256)
@@ -595,39 +618,23 @@
             softmax = sp[rows, lanes] * frow[:, lanes]
             smp[:, lanes] = softmax.astype(BF16)
             dsb[rows, lanes] = (softmax * (grad_probs - drow[:, lanes])).astype(BF16)
-        key_part = nn(dsb[rows, :], qall[...]) * SCALE
-        value_part = nt(smp[...], gtall[...])
-        return key_part, value_part
-
-    own_key = own_value = None
-    for s in range(4):
-        key_part, value_part = backward(s)
-        right_key, right_value = key_part[:128], value_part[:128]
-        left_key, left_value = key_part[128:], value_part[128:]
-        if s > 0:
-            kv_rights[s - 1].wait_recv()
-            right_key = right_key + rrecv_r[s - 1, 0].astype(F32)
-            right_value = right_value + rrecv_r[s - 1, 1].astype(F32)
-        rsend_r[s, 0] = right_key.astype(BF16)
-        rsend_r[s, 1] = right_value.astype(BF16)
-        kv_rights[s].start()
-        pending.append(kv_rights[s])
-        if s < 3:
-            if s > 0:
-                kv_lefts[s - 1].wait_recv()
-                left_key = left_key + rrecv_l[s - 1, 0].astype(F32)
-                left_value = left_value + rrecv_l[s - 1, 1].astype(F32)
-            rsend_l[s, 0] = left_key.astype(BF16)
-            rsend_l[s, 1] = left_value.astype(BF16)
-            kv_lefts[s].start()
-            pending.append(kv_lefts[s])
-        else:
-            own_key, own_value = left_key, left_value
-        if s == 0:
-            for copy in (at_copies[1], at_copies[3], at_far[0], at_far[1]):
-                copy.wait_recv()
-            dwp[...] = nt(at[...], dot2[...])
-        weight_step(s)
+        kvpart[0, rows, :] = nn(dsb[rows, :], qall[...]) * SCALE
+        kvpart[1, rows, :] = nt(smp[...], gtall[...])
+
+    backward(0)
+    kv_sum_rings[0][0](0)
+    backward(1)
+    kv_sum_rings[1][0](0)
+    for copy in (at_copies[1], at_copies[3], at_far[0], at_far[1]):
+        copy.wait_recv()
+    dwp[...] = nt(at[...], dot2[...])
+    for step, _ in dw_rings:
+        step(0)
+    backward(2)
+    backward(3)
+    for s in range(1, 4):
+        for step, _ in kv_sum_rings + dw_rings:
+            step(s)
 
     dq_sem = sems.take(4)
     dq_copies = []
@@ -645,12 +652,8 @@
             dq_copies[-1].start()
     pending += dq_copies
 
-    kv_rights[3].wait_recv()
-    kv_lefts[2].wait_recv()
-    totals = []
-    for i, own in ((0, own_key), (1, own_value)):
-        total = own + rrecv_r[3, i].astype(F32) + rrecv_l[2, i].astype(F32)
-        kvfin_send[i] = total.T.astype(BF16)
+    for i, (_, finish) in enumerate(kv_sum_rings):
+        kvfin_send[i] = finish().T.astype(BF16)
     fin_send = sems.take(4)
     fin_recv = sems.take(4)
     source = lax.rem(yhi - key_quarter + 4, 4)
@@ -679,11 +682,8 @@
     def _():
         kvfin[0] = kvfin_send[:, pl.ds(pl.multiple_of(m * 32, 32), 32), :]
 
-    for i, (rights, lefts) in enumerate(dw_rings):
-        rights[3].wait_recv()
-        lefts[2].wait_recv()
-        total = weight_block(7, i) + wrecv_r[i, 3].astype(F32) + wrecv_l[i, 2].astype(F32)
-        total = total.astype(BF16)
+    for i, (_, finish) in enumerate(dw_rings):
+        total = finish().astype(BF16)
         for y in range(2):
             dwsend[2 * i + y] = total[y * 80 : y * 80 + 80, :]
     dwf_sem = sems.take(4)
@@ -831,20 +831,17 @@
         v((1, 1024), F32),
         v((1, 1024), F32),
         v((256, 1024), BF16),
-        v((4, 2, 128, 128), BF16),
-        v((3, 2, 128, 128), BF16),
-        v((4, 2, 128, 128), BF16),
-        v((3, 2, 128, 128), BF16),
+        v((2, 1024, 128), F32),
+        v((2, 2, 4, 128, 128), BF16),
+        v((2, 2, 4, 128, 128), BF16),
         v((2, 128, 128), BF16),
         v((4, 2, 32, 128), BF16),
         v((4, 128, 256), BF16),
         v((4, 128, 256), BF16),
         v((128, 256), F32),
         v((256, 1280), F32),
-        v((2, 4, 160, 128), BF16),
-        v((2, 3, 160, 128), BF16),
-        v((2, 4, 160, 128), BF16),
-        v((2, 3, 160, 128), BF16),
+        v((2, 2, 4, 160, 128), BF16),
+        v((2, 2, 4, 160, 128), BF16),
         v((4, 80, 128), BF16),
         v((4, 80, 128), BF16),
         pltpu.SemaphoreType.DMA((SEM_COUNT,)),

time: 80.9 us -> 80 us (0.989)
  no operation moved by 1% of the time
where the time goes in v3:
time: 80 us; the launch traced here: 79.8 us
  Pallas kernels  79.2 us (99%)
    pallas_call x1, Pallas kernels, per_device(): pl.pallas_call(kernel, out_shape=(jax.ShapeDtypeStruct((128, 256), BF16),...  77.5 us
    pallas_call x1, Pallas kernels, deliver(): pl.pallas_call(deliver_kernel, out_shape=[jax.ShapeDtypeStruct(r.shape, r...  1.68 us

profile of v3, /device:TPU:6, one launch (start us, length us, event | category | flops | bytes accessed | tf_op | source)
XLA Modules:
  0.0 79.8 jit_solution(6979448782494963142)
XLA Ops:
  0.6 77.5 %shard_map.101 = (bf16[128,256]{1,0:T(8,128)(2,1)}, bf16[128,256]{1,0:T(8,128)(2,1)}, bf16[32,128]{1,0:T(8,128)(2,1)}, bf16[32,128]{1,0:T(8,128)(2,1)}, bf16[8,5120]{1,0:T(8,128)(2,1)}) custom-call(s32[64]{0:T(128)} %order_ref.1, bf16[128,256]{1,0:T(8,128)(2,1)} %q_ref.1, bf16[128,512]{1,0:T(8,128)(2,1)} %k_ref.1, bf16[128,512]{1,0:T(8,128)(2,1)} %v_ref.1, ...), custom_call_target="tpu_custom_call" | custom-call | flops 2500000000 | bytes 1000000 | tf_op jit(solution)/shard_map/pallas_call | solution.py:851
  78.1 1.7 %shard_map.102 = (bf16[128,256]{1,0:T(8,128)(2,1)}, bf16[128,256]{1,0:T(8,128)(2,1)}, bf16[32,128]{1,0:T(8,128)(2,1)}, bf16[32,128]{1,0:T(8,128)(2,1)}, bf16[8,5120]{1,0:T(8,128)(2,1)}) custom-call(bf16[128,256]{1,0:T(8,128)(2,1)} %get-tuple-element.15.refs_0_, bf16[128,256]{1,0:T(8,128)(2,1)} %get-tuple-element.16.refs_1_, ...), custom_call_target="tpu_custom_call" | custom-call | tf_op jit(solution)/shard_map/pallas_call | solution.py:785

commit v4 on v3

--- a/solution.py
+++ b/solution.py
@@ -67,7 +67,7 @@
     wsl, wring, w32, ogt, dot2,
     sp, mx, pb, dsb, mloc,
     osend, obuf, ostat, ostatbuf,
-    at, gpart, gpsend, gpfar, gpnear, gown, gbuf, gstat, gstatbuf, gtall, frow, drow,
+    at, gpart, gpsend, gpbuf, gown, gbuf, gstat, gstatbuf, gtall, frow, drow,
     smp, kvpart, rsend, rrecv, kvfin_send, kvfin,
     dqsend, dqbuf, dqown,
     dwp, wsend, wrecv, dwsend, dwfin,
@@ -144,6 +144,29 @@
     def turn(a):
         return pltpu.roll(a, 64, 1)
 
+    pl.semaphore_wait(
+        barrier, 11 + jnp.where(quarter != yhi, 1, 0) + jnp.where(key_quarter != yhi, 3, 0)
+    )
+
+    def dot_rows(position):
+        return pl.ds(pl.multiple_of(position * 320, 64), 320)
+
+    def dot_lanes(position):
+        return pl.ds(pl.multiple_of(position * TOK, TOK), TOK)
+
+    turn_sem = sems.take(1)
+    turn_copy = sems.copy(
+        ogt, dot2.at[dot_rows(x), dot_lanes(yhi)], turn_sem, turn_sem, *turned
+    )
+
+    @pl.when(quarter != yhi)
+    def _():
+        turn_copy.start()
+
+    @pl.when(quarter == yhi)
+    def _():
+        dot2[dot_rows(x), dot_lanes(yhi)] = ogt[...]
+
     loads[1].wait()
     w_rows = wv[...].astype(F32)
     for half in range(2):
@@ -157,31 +180,6 @@
             odd += [shifted[2], shifted[3], join(shifted[4], w[7]), w[8], w[9]]
         wsl[2 * half] = jnp.concatenate(even, axis=0).astype(BF16)
         wsl[2 * half + 1] = jnp.concatenate(odd, axis=0).astype(BF16)
-    for load in loads[2:]:
-        load.wait()
-
-    pl.semaphore_wait(
-        barrier, 11 + jnp.where(quarter != yhi, 1, 0) + jnp.where(key_quarter != yhi, 3, 0)
-    )
-
-    def dot_rows(position):
-        return pl.ds(pl.multiple_of(position * 320, 64), 320)
-
-    def dot_lanes(position):
-        return pl.ds(pl.multiple_of(position * TOK, TOK), TOK)
-
-    turn_sem = sems.take(1)
-    turn_copy = sems.copy(
-        ogt, dot2.at[dot_rows(x), dot_lanes(yhi)], turn_sem, turn_sem, *turned
-    )
-
-    @pl.when(quarter != yhi)
-    def _():
-        turn_copy.start()
-
-    @pl.when(quarter == yhi)
-    def _():
-        dot2[dot_rows(x), dot_lanes(yhi)] = ogt[...]
 
     w_sem = sems.take(4)
     w_copies = []
@@ -195,6 +193,9 @@
         w_copies[-1].start()
     pending += w_copies
     wring[7, yhi] = wsl[yhi]
+
+    for load in loads[2:]:
+        load.wait()
 
     kv_hop = sems.take(4)
     kv_hop_copies = [
@@ -395,23 +396,15 @@
     heads = (slice(0, 128), slice(128, 256))
     lanes_of = [dot_lanes(lax.rem(yhi + k, 4)) for k in range(4)]
     my_lanes = lanes_of[0]
-    gp_sem = sems.take(6)
-    gp_far, gp_direct, gp_through = [], [], []
-    for way, k in ((0, 1), (1, 3)):
-        gpsend[way] = gpart[heads[way], lanes_of[2]].astype(BF16)
-        gp_far.append(
-            sems.copy(gpsend.at[way], gpfar.at[way], gp_sem + way, gp_sem + way, *y_peer(k))
+    gp_sem = sems.take(4)
+    gp_copies = []
+    for k in (2, 1, 3):
+        gpsend[k] = gpart[:, lanes_of[k]].astype(BF16)
+        gp_copies.append(
+            sems.copy(gpsend.at[k], gpbuf.at[k], gp_sem + k, gp_sem + k, *y_peer(k))
         )
-        gp_far[way].start()
-    for way, k in ((0, 1), (1, 3)):
-        gpsend[2 + way] = gpart[heads[1 - way], lanes_of[k]].astype(BF16)
-        gp_direct.append(
-            sems.copy(
-                gpsend.at[2 + way], gpnear.at[way], gp_sem + 2 + way, gp_sem + 2 + way, *y_peer(k)
-            )
-        )
-        gp_direct[way].start()
-    pending += gp_far + gp_direct
+        gp_copies[-1].start()
+    pending += gp_copies
     ring_step(kv_ring, 4)
     score_block(0)
 
@@ -451,34 +444,13 @@
         o_copies[-2].start()
         o_copies[-1].start()
     pending += o_copies
-    for way, k in ((0, 1), (1, 3)):
-        gp_far[way].wait_recv()
-        gpsend[4 + way] = (
-            gpart[heads[way], lanes_of[k]] + gpfar[way].astype(F32)
-        ).astype(BF16)
-        gp_through.append(
-            sems.copy(
-                gpsend.at[4 + way],
-                gpnear.at[2 + way],
-                gp_sem + 4 + way,
-                gp_sem + 4 + way,
-                *y_peer(k),
-            )
-        )
-        gp_through[way].start()
-    pending += gp_through
-
     own_max, own_sum, own_part = forward(0)
 
-    for copy in gp_direct + gp_through:
-        copy.wait_recv()
-    grad = gpart[:, my_lanes] + jnp.concatenate(
-        [
-            gpnear[1].astype(F32) + gpnear[2].astype(F32),
-            gpnear[0].astype(F32) + gpnear[3].astype(F32),
-        ],
-        axis=0,
-    )
+    for copy in gp_copies:
+        copy.wait_recv()
+    grad = gpart[:, my_lanes]
+    for k in range(1, 4):
+        grad = grad + gpbuf[k].astype(F32)
     grad_bf = grad.astype(BF16)
     gown[...] = grad_bf
     g_sem = sems.take(8)
@@ -820,9 +792,8 @@
         v((4, 8, 256), F32),
         v((256, 512), BF16),
         v((256, 512), F32),
-        v((6, 128, 128), BF16),
-        v((2, 128, 128), BF16),
-        v((4, 128, 128), BF16),
+        v((4, 256, 128), BF16),
+        v((4, 256, 128), BF16),
         v((256, 128), BF16),
         v((4, 256, 128), BF16),
         v((8, 256), F32),

time: 80 us -> 79.8 us (level)
  no operation moved by 1% of the time
where the time goes in v4:
time: 79.8 us; the launch traced here: 79.2 us
  Pallas kernels  78.6 us (98%)
    pallas_call x1, Pallas kernels, per_device(): pl.pallas_call(kernel, out_shape=(jax.ShapeDtypeStruct((128, 256), BF16),...  76.9 us
    pallas_call x1, Pallas kernels, deliver(): pl.pallas_call(deliver_kernel, out_shape=[jax.ShapeDtypeStruct(r.shape, r...  1.68 us

profile of v4, /device:TPU:6, one launch (start us, length us, event | category | flops | bytes accessed | tf_op | source)
XLA Modules:
  0.0 79.2 jit_solution(187707375366912426)
XLA Ops:
  0.6 76.9 %shard_map.101 = (bf16[128,256]{1,0:T(8,128)(2,1)}, bf16[128,256]{1,0:T(8,128)(2,1)}, bf16[32,128]{1,0:T(8,128)(2,1)}, bf16[32,128]{1,0:T(8,128)(2,1)}, bf16[8,5120]{1,0:T(8,128)(2,1)}) custom-call(s32[64]{0:T(128)} %order_ref.1, bf16[128,256]{1,0:T(8,128)(2,1)} %q_ref.1, bf16[128,512]{1,0:T(8,128)(2,1)} %k_ref.1, bf16[128,512]{1,0:T(8,128)(2,1)} %v_ref.1, ...), custom_call_target="tpu_custom_call" | custom-call | flops 2500000000 | bytes 1000000 | tf_op jit(solution)/shard_map/pallas_call | solution.py:822
  77.6 1.7 %shard_map.102 = (bf16[128,256]{1,0:T(8,128)(2,1)}, bf16[128,256]{1,0:T(8,128)(2,1)}, bf16[32,128]{1,0:T(8,128)(2,1)}, bf16[32,128]{1,0:T(8,128)(2,1)}, bf16[8,5120]{1,0:T(8,128)(2,1)}) custom-call(bf16[128,256]{1,0:T(8,128)(2,1)} %get-tuple-element.15.refs_0_, bf16[128,256]{1,0:T(8,128)(2,1)} %get-tuple-element.16.refs_1_, ...), custom_call_target="tpu_custom_call" | custom-call | tf_op jit(solution)/shard_map/pallas_call | solution.py:757

commit v5 on v4

--- a/solution.py
+++ b/solution.py
@@ -98,6 +98,7 @@
     z_left = (node, yhi * 8 + lax.rem(z + 7, 8))
     x_right = ((ylo * 4 + lax.rem(x + 1, 4)) * 2 + core, ctx)
     x_left = ((ylo * 4 + lax.rem(x + 3, 4)) * 2 + core, ctx)
+    x_outer = ((ylo * 4 + lax.rem(x + 3 - 2 * lax.rem(x, 2), 4)) * 2 + core, ctx)
     y_flip = (((1 - ylo) * 4 + x) * 2 + core, ctx)
     sibling = (node + 1 - 2 * core, ctx)
     turned = (((yhi // 2) * 4 + x) * 2 + lax.rem(yhi, 2), quarter * 8 + z)
@@ -123,7 +124,7 @@
     for k in range(1, 4):
         greet(y_peer(k))
         greet(group_peer(k))
-    for peer in (z_right, z_left, x_right, x_left, y_flip):
+    for peer in (z_right, z_left, x_outer, y_flip):
         greet(peer)
 
     @pl.when(quarter != yhi)
@@ -145,7 +146,7 @@
         return pltpu.roll(a, 64, 1)
 
     pl.semaphore_wait(
-        barrier, 11 + jnp.where(quarter != yhi, 1, 0) + jnp.where(key_quarter != yhi, 3, 0)
+        barrier, 10 + jnp.where(quarter != yhi, 1, 0) + jnp.where(key_quarter != yhi, 3, 0)
     )
 
     def dot_rows(position):

time: 79.8 us -> 79.8 us (level)
  no operation moved by 1% of the time
where the time goes in v5:
time: 79.8 us; the launch traced here: 78.8 us
  Pallas kernels  78.1 us (98%)
    pallas_call x1, Pallas kernels, per_device(): pl.pallas_call(kernel, out_shape=(jax.ShapeDtypeStruct((128, 256), BF16),...  76.5 us
    pallas_call x1, Pallas kernels, deliver(): pl.pallas_call(deliver_kernel, out_shape=[jax.ShapeDtypeStruct(r.shape, r...  1.68 us

profile of v5, /device:TPU:6, one launch (start us, length us, event | category | flops | bytes accessed | tf_op | source)
XLA Modules:
  0.0 78.8 jit_solution(61005100762764280)
XLA Ops:
  0.6 76.5 %shard_map.101 = (bf16[128,256]{1,0:T(8,128)(2,1)}, bf16[128,256]{1,0:T(8,128)(2,1)}, bf16[32,128]{1,0:T(8,128)(2,1)}, bf16[32,128]{1,0:T(8,128)(2,1)}, bf16[8,5120]{1,0:T(8,128)(2,1)}) custom-call(s32[64]{0:T(128)} %order_ref.1, bf16[128,256]{1,0:T(8,128)(2,1)} %q_ref.1, bf16[128,512]{1,0:T(8,128)(2,1)} %k_ref.1, bf16[128,512]{1,0:T(8,128)(2,1)} %v_ref.1, ...), custom_call_target="tpu_custom_call" | custom-call | flops 2500000000 | bytes 1000000 | tf_op jit(solution)/shard_map/pallas_call | solution.py:823
  77.1 1.7 %shard_map.102 = (bf16[128,256]{1,0:T(8,128)(2,1)}, bf16[128,256]{1,0:T(8,128)(2,1)}, bf16[32,128]{1,0:T(8,128)(2,1)}, bf16[32,128]{1,0:T(8,128)(2,1)}, bf16[8,5120]{1,0:T(8,128)(2,1)}) custom-call(bf16[128,256]{1,0:T(8,128)(2,1)} %get-tuple-element.15.refs_0_, bf16[128,256]{1,0:T(8,128)(2,1)} %get-tuple-element.16.refs_1_, ...), custom_call_target="tpu_custom_call" | custom-call | tf_op jit(solution)/shard_map/pallas_call | solution.py:758
